TPU v7x, 256 devices: a whole 4x4x8 slice. The times are simulated.
256 devices in a mesh: seg: 64 (over y, z, core), space: 4 (over x).
Axes of the slice: x: 4, y: 4, z: 8, core: 2. Of those that a mesh axis runs over, the one named last changes fastest.
Arguments:
- advect: bfloat16 [64, 4, 4, 256, 512], P('seg', None, 'space'), may hold values from -1 to 1
- growth: bfloat16 [64, 4, 4, 256, 512], P('seg', None, 'space'), may hold values from -0.29882812 to 0.29882812
- forcing: bfloat16 [64, 4, 4, 256, 512], P('seg', None, 'space'), may hold values from -3 to 3
- flux_weight: bfloat16 [64, 4, 4, 256, 512], P('seg', None, 'space'), may hold values from -0.00048828125 to 0.00048828125
- flow_dir: float32 [64, 4, 256, 512], P('seg', 'space'), may hold values from -18 to 18
- helmholtz: float32 [4, 256, 256], P('space'), may hold values from -1 to 2
Outputs:
- multipliers: float32 [64, 4, 256, 512], P('seg', 'space')
- residual: float32 [64, 4, 256, 512], P('seg', 'space')
- sensitivity: float32 [], replicated
All inputs are finite; a program needn't handle non-finite values.
Results may differ from a plain program's by a relative error of at most 0.0005.
Values sent between devices are 32-bit elements; how exact they have to be, the bound alone decides.
A program may use at most 64 MiB of HBM per device.

v0:
```python
import math

import jax
import jax.numpy as jnp
from jax import lax
from jax.sharding import PartitionSpec as P

ITERS = 2


HIGH = lax.Precision.HIGHEST
EPS = 1e-06


def shifted(block, axis, distance):
    devices = range(lax.axis_size(axis))
    route = [(i - distance, i) for i in devices if i - distance in devices]
    return lax.ppermute(block, axis, route)


def fourier_table(width):
    index = jnp.arange(width)
    offset = index[:, None] - index[None, :]
    parity = jnp.where(offset % 2 == 0, 1.0, -1.0).astype(jnp.float32)
    angle = jnp.where(offset == 0, 1, offset).astype(jnp.float32) * (math.pi / width)
    table = 0.5 * parity * jnp.cos(angle) / jnp.sin(angle)
    return jnp.where(offset == 0, 0.0, table)


def derive(field, derivative):
    return jnp.matmul(field, derivative.T, precision=HIGH)


def tangent_sweep(current, advect, growth, helmholtz, derivative, weight, forcing):
    width = derivative.shape[0]
    flux = jnp.float32(0.0)
    for time_step in range(advect.shape[0]):
        speed = advect[time_step].astype(jnp.float32)
        local_rate = growth[time_step].astype(jnp.float32)
        update = current + local_rate * current - speed * derive(current, derivative) / width
        if forcing is not None:
            update = update + forcing[time_step].astype(jnp.float32)
        current = jnp.einsum("mcd,mdx->mcx", helmholtz, update, precision=HIGH)
        flux = flux + jnp.sum(weight[time_step].astype(jnp.float32) * current)
    return (current, flux)


def adjoint_sweep(current, advect, growth, helmholtz, derivative):
    width = derivative.shape[0]
    for time_step in reversed(range(advect.shape[0])):
        pulled = jnp.einsum("mdc,mdx->mcx", helmholtz, current, precision=HIGH)
        speed = advect[time_step].astype(jnp.float32)
        local_rate = growth[time_step].astype(jnp.float32)
        current = pulled + local_rate * pulled + derive(speed * pulled, derivative) / width
    return current


def squares(residual):
    return lax.psum(jnp.sum(residual * residual), ("seg", "space"))


def on_device(advect, growth, forcing, flux_weight, flow_dir, helmholtz):
    advect = advect[0]
    growth = growth[0]
    forcing = forcing[0]
    flux_weight = flux_weight[0]
    flow = flow_dir[0]
    derivative = fourier_table(flow.shape[-1])
    count = lax.axis_size("seg")
    position = lax.axis_index("seg")
    is_last = position == count - 1
    zeros = jnp.zeros_like(flow)
    source_end, source_flux = tangent_sweep(
        zeros, advect, growth, helmholtz, derivative, flux_weight, forcing
    )
    residual = jnp.where(is_last, 0.0, -source_end)
    multipliers = zeros
    direction = residual
    norm_local = jnp.sum(flow * flow)
    flow_norm = lax.psum(norm_local, "space") + EPS
    size_norm = squares(residual)
    sensitivity = source_flux
    for iteration in range(ITERS):
        pulled = adjoint_sweep(direction, advect, growth, helmholtz, derivative)
        before = shifted(direction, "seg", 1)
        joined = pulled - before
        flow_sum = lax.psum(jnp.sum(flow * joined), "space")
        kept = joined - flow_sum / flow_norm * flow
        image, term_flux = tangent_sweep(
            kept, advect, growth, helmholtz, derivative, flux_weight, None
        )
        after = shifted(kept, "seg", -1)
        applied = jnp.where(is_last, 0.0, direction + image - after)
        curvature = lax.psum(jnp.sum(direction * applied), ("seg", "space"))
        step_size = size_norm / curvature
        multipliers = multipliers + step_size * direction
        residual = residual - step_size * applied
        sensitivity = sensitivity + step_size * term_flux
        if iteration + 1 < ITERS:
            fresh = squares(residual)
            direction = residual + fresh / size_norm * direction
            size_norm = fresh
    total = lax.psum(sensitivity, ("seg", "space"))
    return (multipliers[None], residual[None], total)


def solution(mesh):
    in_specs = (
        P("seg", None, "space", None, None),
        P("seg", None, "space", None, None),
        P("seg", None, "space", None, None),
        P("seg", None, "space", None, None),
        P("seg", "space", None, None),
        P("space", None, None),
    )
    out_specs = (P("seg", "space", None, None), P("seg", "space", None, None), P())
    return jax.shard_map(
        on_device, mesh=mesh, in_specs=in_specs, out_specs=out_specs, check_vma=False
    )
```

profile of v0, /device:TPU:1, one launch (start us, length us, event | category | flops | bytes accessed | tf_op | source)
XLA Modules:
  0.0 535.6 jit_solution(6908121653630086912)
XLA Ops:
  7.6 6.5 %fusion.37 = f32[256,512]{0,1:T(8,128)S(1)} fusion(bf16[1,1,1,256,512]{3,4,2,1,0:T(8,128)(2,1)S(1)} %copy.36, bf16[1,1,1,256,512]{3,4,2,1,0:T(8,128)(2,1)S(1)} %copy.38, bf16[1,1,1,256,512]{3,4,2,1,0:T(8,128)(2,1)S(1)} %copy-done.46), kind=kOutput, calls=%fused_computation.72 | convolution fusion | flops 812122112 | bytes 1310720 | tf_op jit(solution)/shard_map/dot_general | solution.py:31
  15.6 8.0 %fusion.35 = f32[256,512]{0,1:T(8,128)S(1)} fusion(f32[512,256]{1,0:T(8,128)S(1)} %fusion.129, bf16[1,1,1,256,512]{3,4,2,1,0:T(8,128)(2,1)S(1)} %copy.41, bf16[1,1,1,256,512]{3,4,2,1,0:T(8,128)(2,1)S(1)} %copy-done.37, bf16[1,1,1,256,512]{3,4,2,1,0:T(8,128)(2,1)S(1)} %copy-done.42), kind=kOutput, calls=%fused_computation.70 | convolution fusion | flops 812253184 | bytes 1835008 | tf_op jit(solution)/shard_map/dot_general | solution.py:31
  25.1 8.0 %fusion.33 = f32[256,512]{0,1:T(8,128)S(1)} fusion(f32[512,256]{1,0:T(8,128)S(1)} %fusion.127, bf16[1,1,1,256,512]{3,4,2,1,0:T(8,128)(2,1)S(1)} %copy.44, bf16[1,1,1,256,512]{3,4,2,1,0:T(8,128)(2,1)S(1)} %copy.43, bf16[1,1,1,256,512]{3,4,2,1,0:T(8,128)(2,1)S(1)} %copy-done.32), kind=kOutput, calls=%fused_computation.68 | convolution fusion | flops 812253184 | bytes 1835008 | tf_op jit(solution)/shard_map/dot_general | solution.py:31
  34.6 8.0 %fusion.31 = f32[256,512]{0,1:T(8,128)S(1)} fusion(f32[512,256]{1,0:T(8,128)S(1)} %fusion.125, bf16[1,1,1,256,512]{3,4,2,1,0:T(8,128)(2,1)S(1)} %copy.47, bf16[1,1,1,256,512]{3,4,2,1,0:T(8,128)(2,1)S(1)} %copy.46, bf16[1,1,1,256,512]{3,4,2,1,0:T(8,128)(2,1)S(1)} %copy.45), kind=kOutput, calls=%fused_computation.66 | convolution fusion | flops 812253184 | bytes 1835008 | tf_op jit(solution)/shard_map/dot_general | solution.py:31
  46.4 5.5 %collective-permute-start = (f32[1,256,512]{1,2,0:T(8,128)}, f32[1,256,512]{1,2,0:T(8,128)}, u32[]{:S(2)}, u32[]{:S(2)}) collective-permute-start(f32[1,256,512]{1,2,0:T(8,128)} %get-tuple-element.43), channel_id=1, source_target_pairs={{0,4},{4,8},{8,12},{12,16},{16,20},{20,24},{24,28},{28,32},{32,36}... | collective-permute-start | bytes 1572872 | tf_op jit(solution)/shard_map/ppermute | solution.py:18
  52.8 6.2 %fusion.4 = f32[256,512]{0,1:T(8,128)S(1)} fusion(f32[256,512]{0,1:T(8,128)S(1)} %convolution_bitcast_fusion.8, bf16[1,1,1,256,512]{3,4,2,1,0:T(8,128)(2,1)} %copy-done.21, bf16[1,1,1,256,512]{3,4,2,1,0:T(8,128)(2,1)} %copy-done.24), kind=kOutput, calls=%fused_computation.29 | convolution fusion | flops 811991040 | bytes 1572864 | tf_op jit(solution)/shard_map/dot_general | solution.py:31
  60.0 5.3 fusion.5
  67.7 6.1 %fusion.6 = f32[256,512]{0,1:T(8,128)S(1)} fusion(f32[256,512]{0,1:T(8,128)S(1)} %convolution_bitcast_fusion.6, bf16[1,1,1,256,512]{3,4,2,1,0:T(8,128)(2,1)S(1)} %copy-done.38, bf16[1,1,1,256,512]{3,4,2,1,0:T(8,128)(2,1)} %copy.39), kind=kOutput, calls=%fused_computation.31 | convolution fusion | flops 811991040 | bytes 1572864 | tf_op jit(solution)/shard_map/dot_general | solution.py:31
  74.8 7.3 %fusion.91 = (f32[]{:T(128)}, f32[]{:T(128)}, f32[1,256,512]{1,2,0:T(8,128)S(1)}) fusion(f32[1,1,256,512]{2,3,1,0:T(8,128)S(1)} %copy.22, f32[1,256,512]{1,2,0:T(8,128)} %collective-permute-done, f32[256,512]{0,1:T(8,128)S(1)} %convolution_bitcast_fusion.5, bf16[1,1,1,256,512]{3,4,2,1,0:T(8,128)(2,1)S(1)} %copy-done.47, ...), kind=kOutput, calls=%fused_computation.175 | convolution fusion | flops 812646400 | bytes 2621448 | tf_op jit(solution)/shard_map/dot_general | solution.py:31
  82.1 9.1 %all-reduce.1 = (f32[]{:T(128)}, f32[]{:T(128)}) all-reduce(f32[]{:T(128)} %get-tuple-element.9, f32[]{:T(128)} %get-tuple-element.8), channel_id=1, replica_groups=mesh['seg'=64,'space'=4] {'space'}, use_global_device_ids=true, to_apply=%region_3.4 | all-reduce | flops 2 | bytes 16 | tf_op jit(solution)/shard_map/psum | solution.py:87
  93.5 8.0 %fusion.10 = f32[1,256,512]{1,2,0:T(8,128)S(1)} fusion(f32[1,256,512]{1,2,0:T(8,128)S(1)} %fusion.92, bf16[1,1,1,256,512]{3,4,2,1,0:T(8,128)(2,1)S(1)} %copy-done.48), kind=kOutput, calls=%fused_computation.35 | convolution fusion | flops 811466752 | bytes 1310720 | tf_op jit(solution)/shard_map/dot_general | solution.py:31
  106.3 8.0 %fusion.29 = f32[256,512]{0,1:T(8,128)S(1)} fusion(f32[512,256]{1,0:T(8,128)S(1)} %fusion.65, bf16[1,1,1,256,512]{3,4,2,1,0:T(8,128)(2,1)S(1)} %copy-done.39, bf16[1,1,1,256,512]{3,4,2,1,0:T(8,128)(2,1)S(1)} %copy-done.43), kind=kOutput, calls=%fused_computation.64 | convolution fusion | flops 811991040 | bytes 1572864 | tf_op jit(solution)/shard_map/dot_general | solution.py:31
  115.8 8.0 %fusion.28 = f32[256,512]{0,1:T(8,128)S(1)} fusion(f32[512,256]{1,0:T(8,128)S(1)} %fusion.117, bf16[1,1,1,256,512]{3,4,2,1,0:T(8,128)(2,1)S(1)} %copy-done.29, bf16[1,1,1,256,512]{3,4,2,1,0:T(8,128)(2,1)S(1)} %copy-done.34), kind=kOutput, calls=%fused_computation.63 | convolution fusion | flops 811991040 | bytes 1572864 | tf_op jit(solution)/shard_map/dot_general | solution.py:31
  124.8 8.0 %fusion.27 = f32[256,512]{0,1:T(8,128)S(1)} fusion(f32[512,256]{1,0:T(8,128)S(1)} %fusion.115, bf16[1,1,1,256,512]{3,4,2,1,0:T(8,128)(2,1)S(1)} %copy-done.22, bf16[1,1,1,256,512]{3,4,2,1,0:T(8,128)(2,1)S(1)} %copy-done.25), kind=kOutput, calls=%fused_computation.62 | convolution fusion | flops 811991040 | bytes 1572864 | tf_op jit(solution)/shard_map/dot_general | solution.py:31
  134.1 78.0 %all-reduce = (f32[]{:T(128)}, f32[]{:T(128)}) all-reduce(f32[]{:T(128)} %get-tuple-element.7, f32[]{:T(128)} %get-tuple-element.45), channel_id=1, replica_groups=mesh['seg'=64,'space'=4] {'seg','space'}, use_global_device_ids=true, to_apply=%region_1.2 | all-reduce | flops 2 | bytes 16 | tf_op jit(solution)/shard_map/psum | solution.py:59
  215.3 73.5 %psum.60 = f32[]{:T(128)} all-reduce(f32[]{:T(128)} %multiply_reduce_fusion.1), channel_id=1, replica_groups=mesh['seg'=64,'space'=4] {'seg','space'}, use_global_device_ids=true, to_apply=%region_9.10 | all-reduce | flops 1 | bytes 8 | tf_op jit(solution)/shard_map/psum | solution.py:59
  314.1 7.1 %fusion.93 = (f32[]{:T(128)}, f32[1,256,512]{1,2,0:T(8,128)}) fusion(f32[1,1,256,512]{2,3,1,0:T(8,128)S(1)} %copy.22, f32[1,256,512]{1,2,0:T(8,128)S(1)} %collective-permute-done.2, f32[256,512]{0,1:T(8,128)S(1)} %convolution_bitcast_fusion, bf16[1,1,1,256,512]{3,4,2,1,0:T(8,128)(2,1)S(1)} %copy-done.49, bf16[1,1,1,256,512]{3,4,2,1,0:T(8,128)(2,1)S(1)} %copy.36), kind=kOutput, calls=%fused_computation.177 | convolution fusion | flops 812384256 | bytes 2621444 | tf_op jit(solution)/shard_map/dot_general | solution.py:31
  321.2 9.1 %psum.61 = f32[]{:T(128)} all-reduce(f32[]{:T(128)} %get-tuple-element.47), channel_id=1, replica_groups=mesh['seg'=64,'space'=4] {'space'}, use_global_device_ids=true, to_apply=%region_11.12 | all-reduce | flops 1 | bytes 8 | tf_op jit(solution)/shard_map/psum | solution.py:87
  332.9 6.3 %fusion.20 = f32[1,256,512]{1,2,0:T(8,128)S(1)} fusion(f32[1,256,512]{1,2,0:T(8,128)} %fusion.94, bf16[1,1,1,256,512]{3,4,2,1,0:T(8,128)(2,1)S(1)} %copy-done.50), kind=kOutput, calls=%fused_computation.45 | convolution fusion | flops 811466752 | bytes 1310720 | tf_op jit(solution)/shard_map/dot_general | solution.py:31
  343.9 8.0 %fusion.26 = f32[256,512]{0,1:T(8,128)S(1)} fusion(f32[512,256]{1,0:T(8,128)S(1)} %get-tuple-element.51, bf16[1,1,1,256,512]{3,4,2,1,0:T(8,128)(2,1)S(1)} %copy-done.41, bf16[1,1,1,256,512]{3,4,2,1,0:T(8,128)(2,1)S(1)} %copy-done.45), kind=kOutput, calls=%fused_computation.61 | convolution fusion | flops 811991040 | bytes 1572864 | tf_op jit(solution)/shard_map/dot_general | solution.py:31
  353.4 8.0 %fusion.25 = f32[256,512]{0,1:T(8,128)S(1)} fusion(f32[512,256]{1,0:T(8,128)S(1)} %get-tuple-element.52, bf16[1,1,1,256,512]{3,4,2,1,0:T(8,128)(2,1)S(1)} %copy-done.31, bf16[1,1,1,256,512]{3,4,2,1,0:T(8,128)(2,1)S(1)} %copy-done.36), kind=kOutput, calls=%fused_computation.60 | convolution fusion | flops 811991040 | bytes 1572864 | tf_op jit(solution)/shard_map/dot_general | solution.py:31
  369.1 8.8 %fusion.24 = f32[256,512]{0,1:T(8,128)S(1)} fusion(f32[512,256]{1,0:T(8,128)S(1)} %get-tuple-element.53, bf16[1,1,1,256,512]{3,4,2,1,0:T(8,128)(2,1)} %copy-done.21, bf16[1,1,1,256,512]{3,4,2,1,0:T(8,128)(2,1)} %copy-done.24), kind=kOutput, calls=%fused_computation.59 | convolution fusion | flops 811991040 | bytes 1572864 | tf_op jit(solution)/shard_map/dot_general | solution.py:31
  380.3 73.9 %psum.62 = f32[]{:T(128)} all-reduce(f32[]{:T(128)} %get-tuple-element.49), channel_id=1, replica_groups=mesh['seg'=64,'space'=4] {'seg','space'}, use_global_device_ids=true, to_apply=%region_13.14 | all-reduce | flops 1 | bytes 8 | tf_op jit(solution)/shard_map/psum | solution.py:94
  457.7 72.6 %psum.63 = f32[]{:T(128)} all-reduce(f32[]{:T(128)S(6)} %add.287), channel_id=1, replica_groups=mesh['seg'=64,'space'=4] {'seg','space'}, use_global_device_ids=true, to_apply=%region_26.27 | all-reduce | flops 1 | bytes 8 | tf_op jit(solution)/shard_map/psum | solution.py:103
  (162 shorter events, 72.3 us)
Async XLA Ops:
  0.6 13.5 %copy-start = (f32[1,256,256]{2,1,0:T(8,128)S(1)}, f32[1,256,256]{2,1,0:T(8,128)}, u32[]{:S(2)}) copy-start(f32[1,256,256]{2,1,0:T(8,128)} %param.11) | copy-start | bytes 786436
  2.1 31.7 %copy-start.21 = (bf16[1,1,1,256,512]{3,4,2,1,0:T(8,128)(2,1)}, bf16[1,1,1,256,512]{3,4,2,1,0:T(8,128)(2,1)S(1)}, u32[]{:S(2)}) copy-start(bf16[1,1,1,256,512]{3,4,2,1,0:T(8,128)(2,1)S(1)} %copy.46) | copy-start | bytes 786436
  2.3 22.0 %copy-start.27 = (bf16[1,1,1,256,512]{3,4,2,1,0:T(8,128)(2,1)}, bf16[1,1,1,256,512]{3,4,2,1,0:T(8,128)(2,1)S(1)}, u32[]{:S(2)}) copy-start(bf16[1,1,1,256,512]{3,4,2,1,0:T(8,128)(2,1)S(1)} %copy.43) | copy-start | bytes 786436
  4.2 29.5 %copy-start.24 = (bf16[1,1,1,256,512]{3,4,2,1,0:T(8,128)(2,1)}, bf16[1,1,1,256,512]{3,4,2,1,0:T(8,128)(2,1)S(1)}, u32[]{:S(2)}) copy-start(bf16[1,1,1,256,512]{3,4,2,1,0:T(8,128)(2,1)S(1)} %copy.45) | copy-start | bytes 786436
  46.4 6.1 %copy-start.20 = (f32[1,1,256,512]{3,2,1,0:T(8,128)S(1)}, f32[1,1,256,512]{3,2,1,0:T(8,128)}, u32[]{:S(2)}) copy-start(f32[1,1,256,512]{3,2,1,0:T(8,128)} %param.10) | copy-start | bytes 1572868
  46.4 28.0 %collective-permute-start = (f32[1,256,512]{1,2,0:T(8,128)}, f32[1,256,512]{1,2,0:T(8,128)}, u32[]{:S(2)}, u32[]{:S(2)}) collective-permute-start(f32[1,256,512]{1,2,0:T(8,128)} %get-tuple-element.43), channel_id=1, source_target_pairs={{0,4},{4,8},{8,12},{12,16},{16,20},{20,24},{24,28},{28,32},{32,36}... | collective-permute-start | bytes 1572872 | tf_op jit(solution)/shard_map/ppermute | solution.py:18
  101.5 4.8 copy-start.39
  101.5 4.8 copy-start.43
  101.5 31.4 %collective-permute-start.1 = (f32[1,256,512]{1,2,0:T(8,128)S(1)}, f32[1,256,512]{1,2,0:T(8,128)S(1)}, u32[]{:S(2)}, u32[]{:S(2)}) collective-permute-start(f32[1,256,512]{1,2,0:T(8,128)S(1)} %fusion.92), channel_id=1, source_target_pairs={{4,0},{8,4},{12,8},{16,12},{20,16},{24,20},{28,24},{32,28},{36,32}... | collective-permute-start | bytes 1572872 | tf_op jit(solution)/shard_map/ppermute | solution.py:18
  124.8 8.0 %copy-start.7 = (f32[512,256]{1,0:T(8,128)}, f32[512,256]{1,0:T(8,128)S(1)}, u32[]{:S(2)}) copy-start(f32[512,256]{1,0:T(8,128)S(1)} %fusion.115) | copy-start | bytes 1572868
  290.4 5.1 copy-start.23
  290.4 5.1 copy-start.26
  291.0 22.7 %collective-permute-start.2 = (f32[1,256,512]{1,2,0:T(8,128)S(1)}, f32[1,256,512]{1,2,0:T(8,128)S(1)}, u32[]{:S(2)}, u32[]{:S(2)}) collective-permute-start(f32[1,256,512]{1,2,0:T(8,128)S(1)} %bitcast_add_fusion.1), channel_id=1, source_target_pairs={{0,4},{4,8},{8,12},{12,16},{16,20},{20,24},{24,28},{28,32},{32,36}... | collective-permute-start | bytes 1572872 | tf_op jit(solution)/shard_map/ppermute | solution.py:18
  332.9 8.6 %copy-start.6 = (f32[512,256]{1,0:T(8,128)S(1)}, f32[512,256]{1,0:T(8,128)}, u32[]{:S(2)}) copy-start(f32[512,256]{1,0:T(8,128)} %copy-done.5) | copy-start | bytes 1572868
  332.9 8.6 %copy-start.12 = (f32[512,256]{1,0:T(8,128)S(1)}, f32[512,256]{1,0:T(8,128)}, u32[]{:S(2)}) copy-start(f32[512,256]{1,0:T(8,128)} %copy-done.11) | copy-start | bytes 1572868
  332.9 8.6 %copy-start.19 = (bf16[1,1,1,256,512]{3,4,2,1,0:T(8,128)(2,1)S(1)}, bf16[1,1,1,256,512]{3,4,2,1,0:T(8,128)(2,1)}, u32[]{:S(2)}) copy-start(bf16[1,1,1,256,512]{3,4,2,1,0:T(8,128)(2,1)} %copy.48) | copy-start | bytes 786436
  339.2 4.7 copy-start.41
  339.2 38.8 %collective-permute-start.3 = (f32[1,256,512]{1,2,0:T(8,128)}, f32[1,256,512]{1,2,0:T(8,128)}, u32[]{:S(2)}, u32[]{:S(2)}) collective-permute-start(f32[1,256,512]{1,2,0:T(8,128)} %fusion.94), channel_id=1, source_target_pairs={{4,0},{8,4},{12,8},{16,12},{20,16},{24,20},{28,24},{32,28},{36,32}... | collective-permute-start | bytes 1572872 | tf_op jit(solution)/shard_map/ppermute | solution.py:18
  343.9 8.1 %copy-start.4 = (f32[512,256]{1,0:T(8,128)S(1)}, f32[512,256]{1,0:T(8,128)}, u32[]{:S(2)}) copy-start(f32[512,256]{1,0:T(8,128)} %copy-done.3) | copy-start | bytes 1572868
  343.9 8.1 %copy-start.10 = (f32[512,256]{1,0:T(8,128)S(1)}, f32[512,256]{1,0:T(8,128)}, u32[]{:S(2)}) copy-start(f32[512,256]{1,0:T(8,128)} %copy-done.9) | copy-start | bytes 1572868
  343.9 8.1 %copy-start.17 = (bf16[1,1,1,256,512]{3,4,2,1,0:T(8,128)(2,1)S(1)}, bf16[1,1,1,256,512]{3,4,2,1,0:T(8,128)(2,1)}, u32[]{:S(2)}) copy-start(bf16[1,1,1,256,512]{3,4,2,1,0:T(8,128)(2,1)} %copy.49) | copy-start | bytes 786436
  353.3 8.1 %copy-start.2 = (f32[512,256]{1,0:T(8,128)S(1)}, f32[512,256]{1,0:T(8,128)}, u32[]{:S(2)}) copy-start(f32[512,256]{1,0:T(8,128)} %copy-done.1) | copy-start | bytes 1572868
  353.3 8.1 %copy-start.8 = (f32[512,256]{1,0:T(8,128)S(1)}, f32[512,256]{1,0:T(8,128)}, u32[]{:S(2)}) copy-start(f32[512,256]{1,0:T(8,128)} %copy-done.7) | copy-start | bytes 1572868
  353.3 8.1 %copy-start.16 = (bf16[1,1,1,256,512]{3,4,2,1,0:T(8,128)(2,1)S(1)}, bf16[1,1,1,256,512]{3,4,2,1,0:T(8,128)(2,1)}, u32[]{:S(2)}) copy-start(bf16[1,1,1,256,512]{3,4,2,1,0:T(8,128)(2,1)} %copy.50) | copy-start | bytes 786436
  (31 other events, 39.4 us)
where the time goes:
time: 543 us; the launch traced here: 536 us
  blocking collectives  316 us (58%)
  matrix products  159 us (29%)
  local copies, waits for them, and re-layouts  21.6 us (4%)
  starting transfers between devices  15.7 us (3%)
  between operations  15.7 us (3%)
  other arithmetic  7.42 us (1%)
    psum x2, blocking collectives, squares(): return lax.psum(jnp.sum(residual * residual), ('seg', 'space'))  151 us
    dot_general x20, matrix products, derive(): return jnp.matmul(field, derivative.T, precision=HIGH)  141 us
    psum x1, blocking collectives, on_device(): curvature = lax.psum(jnp.sum(direction * applied), ('seg', 'space'))  73.9 us
    psum x1, blocking collectives, on_device(): total = lax.psum(sensitivity, ('seg', 'space'))  72.6 us
    unnamed x121, local copies, waits for them, and re-layouts  19.3 us
    psum x2, blocking collectives, on_device(): flow_sum = lax.psum(jnp.sum(flow * joined), 'space')  18.2 us
    ppermute x4, starting transfers between devices, shifted(): return lax.ppermute(block, axis, route)  15.7 us
    dot_general x12, matrix products, tangent_sweep(): current = jnp.einsum('mcd,mdx->mcx', helmholtz, update, precision=HIGH)  12.9 us
  transfers between devices with their start and end apart: 4, of which 0 were waited for; matrix products, arithmetic and copies ran while one was open for 18% of the time, Pallas kernels for 0%

commit v1 on v0

v1 whole, which is shorter than its diff:
```python
import functools
import math

import jax
import jax.numpy as jnp
import numpy as np
from jax import lax
from jax.experimental import pallas as pl
from jax.experimental.pallas import tpu as pltpu
from jax.sharding import PartitionSpec as P

EPS = 1e-06
F32 = jnp.float32
BF16 = jnp.bfloat16
MESH = pl.DeviceIdType.MESH
CHUNKS = 4


def derivative_tables(width):
    offset = np.arange(width)
    angle = np.where(offset == 0, 1, offset) * (math.pi / width)
    wave = 0.5 * np.where(offset % 2 == 0, 1.0, -1.0) / np.tan(angle) / width
    wave[0] = 0.0
    half = width // 2
    index = np.arange(half)
    apart = index[None, :] - index[:, None]
    near, far = wave[apart % width], wave[(apart + half) % width]
    pieces = []
    for table in (0.5 * (near + far), 0.5 * (near - far)):
        high = table.astype(np.float32).astype(jnp.bfloat16)
        pieces += [high, (table - high.astype(np.float64)).astype(np.float32).astype(jnp.bfloat16)]
    return np.stack(pieces)


def dot(a, b):
    return jnp.dot(a, b, preferred_element_type=F32)


def split(x):
    high = x.astype(BF16)
    return high, (x - high.astype(F32)).astype(BF16)


def derive(field, tables):
    half = field.shape[1] // 2
    left, right = field[:, :half], field[:, half:]
    sum_high, sum_low = split(left + right)
    gap_high, gap_low = split(left - right)
    even = dot(sum_high, tables[0]) + dot(sum_low, tables[0]) + dot(sum_high, tables[1])
    odd = dot(gap_high, tables[2]) + dot(gap_low, tables[2]) + dot(gap_high, tables[3])
    return jnp.concatenate([even + odd, even - odd], axis=1)


def mix(matrix, field):
    high, low = split(field)
    return dot(matrix[0], high) + dot(matrix[1], high) + dot(matrix[0], low)


def lanes(product):
    row = jnp.sum(product, axis=0, keepdims=True)
    return sum(row[:, k : k + 128] for k in range(0, row.shape[1], 128))


def total(row):
    return jnp.sum(row, axis=1, keepdims=True)


def kernel(
    groups, advect_in, growth_in, forcing_in, weight_in, flow_in, helm_in, tables_in,
    mult_out, res_out, sens_out,
    advect, growth, forcing, weight, flow, helm, tables, matrix,
    state, p0, w0, y0, s1, w1, tang_flow, grad, v1,
    flow_next, p_prev, w0_next, y_prev, w1_next,
    near_own, near_next, plane, line, line_next,
    load_sem, send_sem, recv_sem,
    near_send, near_recv, next_recv, plane_send, plane_recv, line_send, line_recv, line_next_sem,
):
    seg_count, space_count, rows = groups
    seg, space = lax.axis_index("seg"), lax.axis_index("space")
    after, before = lax.rem(seg + 1, seg_count), lax.rem(seg + seg_count - 1, seg_count)
    steps, height, width = advect.shape
    planes = seg_count // rows
    active = jnp.where(seg < seg_count - 1, 1.0, 0.0).astype(F32)
    not_first = jnp.where(seg > 0, 1.0, 0.0).astype(F32)

    def load(slot, source, target):
        return pltpu.make_async_copy(source, target, load_sem.at[slot])

    def step_loads(n):
        return (
            load(n, forcing_in.at[n], forcing.at[n]),
            load(steps + n, advect_in.at[n], advect.at[n]),
            load(2 * steps + n, growth_in.at[n], growth.at[n]),
        )

    base = 3 * steps
    load_helm = load(base, helm_in, helm)
    load_tables = load(base + 1, tables_in, tables)
    load_flow = load(base + 2, flow_in, flow)
    load_weight = load(base + 3, weight_in, weight)
    load_helm.start()
    step_loads(0)[0].start()
    load_tables.start()
    for n in range(1, steps):
        for copy in step_loads(n):
            copy.start()
    for copy in step_loads(0)[1:]:
        copy.start()
    load_flow.start()
    load_weight.start()

    plane_me = (seg // rows) * space_count + space
    line_me = lax.rem(seg, rows)
    plane_size, line_size = planes * space_count, rows

    def plane_peer(d):
        j = lax.rem(plane_me + d, plane_size)
        return j, (lax.div(j, space_count) * rows + line_me, lax.rem(j, space_count))

    def line_peer(d):
        j = lax.rem(line_me + d, line_size)
        return j, ((seg // rows) * rows + j, space)

    barrier = pltpu.get_barrier_semaphore()
    greeted = [plane_peer(d)[1] for d in range(1, plane_size)]
    greeted += [line_peer(d)[1] for d in range(1, line_size)]
    greeted += [(s, lax.rem(space + d, space_count)) for s in (before, after) for d in range(space_count)]
    for peer in greeted:
        pl.semaphore_signal(barrier, inc=1, device_id=peer, device_id_type=MESH)

    piece = height // CHUNKS

    def transfer(kind, source, target, seg_to):
        return [
            pltpu.make_async_remote_copy(
                src_ref=source.at[pl.ds(c * piece, piece), :],
                dst_ref=target.at[pl.ds(c * piece, piece), :],
                send_sem=send_sem.at[kind, c],
                recv_sem=recv_sem.at[kind, c],
                device_id=(seg_to, space),
                device_id_type=MESH,
            )
            for c in range(CHUNKS)
        ]

    def start(copies):
        for copy in copies:
            copy.start()

    def arrived(copies):
        for copy in copies:
            copy.wait_recv()

    send_flow = transfer(0, flow_in, flow_next, before)
    send_p0 = transfer(1, p0, p_prev, after)
    send_w0 = transfer(2, w0, w0_next, before)
    send_y0 = transfer(3, y0, y_prev, after)
    send_w1 = transfer(4, w1, w1_next, before)

    def spread(d_table):
        return [tables[k] for k in range(4)]

    def forward():
        return matrix[0], matrix[1]

    def backward():
        return matrix[2], matrix[3]

    def tangent_step(n, forced):
        now = state[...]
        rate = growth[n].astype(F32)
        speed = advect[n].astype(F32)
        update = now + rate * now - speed * derive(now, spread(0))
        if forced:
            update = update + forcing[n].astype(F32)
        state[...] = mix(forward(), update)

    def adjoint_rest(n, pulled):
        rate = growth[n].astype(F32)
        speed = advect[n].astype(F32)
        return pulled + rate * pulled + derive(speed * pulled, spread(0))

    def tangent_sweep(first, last):
        @pl.loop(first, last)
        def _(n):
            tangent_step(n, False)

    def adjoint_sweep():
        @pl.loop(0, steps)
        def _(k):
            state[...] = adjoint_rest(steps - 1 - k, mix(backward(), state[...]))

    load_helm.wait()
    high, low = split(helm[...])
    matrix[0], matrix[1] = high, low
    high, low = split(helm[...].T)
    matrix[2], matrix[3] = high, low
    step_loads(0)[0].wait()
    state[...] = dot(matrix[0], forcing[0]) + dot(matrix[1], forcing[0])
    pl.semaphore_wait(barrier, len(greeted))
    start(send_flow)
    load_tables.wait()

    @pl.loop(1, steps)
    def _(n):
        for copy in step_loads(n):
            copy.wait()
        tangent_step(n, True)

    p0[...] = -active * state[...]
    start(send_p0)

    for copy in step_loads(0)[1:]:
        copy.wait()
    state[...] = p0[...]
    adjoint_sweep()
    w0[...] = state[...]
    start(send_w0)

    load_flow.wait()
    state[...] = flow[...]
    tangent_sweep(0, steps)
    tang_flow[...] = state[...]

    load_weight.wait()
    state[...] = jnp.zeros_like(state)

    def gradient_step(k, flux):
        n = steps - 1 - k
        pulled = mix(backward(), weight[n].astype(F32) + state[...])
        state[...] = adjoint_rest(n, pulled)
        return flux + lanes(pulled * forcing[n].astype(F32))

    flux_row = lax.fori_loop(0, steps, gradient_step, jnp.zeros((1, 128), F32))
    grad[...] = state[...]

    ff_row = lanes(flow[...] * flow[...])
    gf_row = lanes(grad[...] * flow[...])
    pp_row = lanes(p0[...] * p0[...])

    arrived(send_p0)
    state[...] = w0[...] - p_prev[...]
    fv0_row = lanes(flow[...] * state[...])
    near_own[space] = jnp.concatenate([ff_row, fv0_row, jnp.zeros((6, 128), F32)], axis=0)
    near_copies = []
    for d in range(1, space_count):
        j = lax.rem(space + d, space_count)
        near_copies.append(
            (
                pltpu.make_async_remote_copy(
                    src_ref=near_own.at[space], dst_ref=near_own.at[space], send_sem=near_send.at[d - 1],
                    recv_sem=near_recv.at[space], device_id=(seg, j), device_id_type=MESH,
                ),
                pltpu.make_async_remote_copy(
                    src_ref=near_own.at[j], dst_ref=near_own.at[j], send_sem=near_send.at[d - 1],
                    recv_sem=near_recv.at[j], device_id=(seg, j), device_id_type=MESH,
                ),
            )
        )
    for d in range(space_count):
        j = lax.rem(space + d, space_count)
        near_copies.append(
            (
                pltpu.make_async_remote_copy(
                    src_ref=near_own.at[space], dst_ref=near_next.at[space],
                    send_sem=near_send.at[space_count - 1 + d], recv_sem=next_recv.at[space],
                    device_id=(before, j), device_id_type=MESH,
                ),
                pltpu.make_async_remote_copy(
                    src_ref=near_own.at[j], dst_ref=near_next.at[j],
                    send_sem=near_send.at[space_count - 1 + d], recv_sem=next_recv.at[j],
                    device_id=(before, j), device_id_type=MESH,
                ),
            )
        )
    for copy, _ in near_copies:
        copy.start()
    vv0_row = lanes(state[...] * state[...])
    gv0_row = lanes(grad[...] * state[...])
    tangent_sweep(0, steps)
    for _, copy in near_copies:
        copy.wait_recv()
    sums = near_own[0] + near_own[1] + near_own[2] + near_own[3]
    c0 = total(sums[1:2]) / (total(sums[0:1]) + EPS)
    sums = near_next[0] + near_next[1] + near_next[2] + near_next[3]
    c0_next = total(sums[1:2]) / (total(sums[0:1]) + EPS)
    y0[...] = state[...] - c0 * tang_flow[...]
    start(send_y0)

    arrived(send_w0)
    arrived(send_flow)
    s1[...] = active * (2.0 * p0[...] + y0[...] - w0_next[...] + c0_next * flow_next[...])
    state[...] = s1[...]
    adjoint_sweep()
    w1[...] = state[...]
    start(send_w1)
    ss_row = lanes(s1[...] * s1[...])

    arrived(send_y0)
    state[...] = w1[...] - not_first * (2.0 * p_prev[...] + y_prev[...] - w0[...] + c0 * flow[...])
    v1_rows = [lanes(other * state[...]) for other in (flow[...], state[...], grad[...])]
    plane[plane_me] = jnp.concatenate(
        [ff_row, gf_row, fv0_row, vv0_row, gv0_row, *v1_rows, pp_row, ss_row, flux_row, jnp.zeros((5, 128), F32)],
        axis=0,
    )

    def plane_copy(d):
        j, peer = plane_peer(d)
        send = pltpu.make_async_remote_copy(
            src_ref=plane.at[plane_me], dst_ref=plane.at[plane_me], send_sem=plane_send.at[d],
            recv_sem=plane_recv.at[plane_me], device_id=peer, device_id_type=MESH,
        )
        receive = pltpu.make_async_remote_copy(
            src_ref=plane.at[j], dst_ref=plane.at[j], send_sem=plane_send.at[d],
            recv_sem=plane_recv.at[j], device_id=peer, device_id_type=MESH,
        )
        return send, receive

    plane_copies = [plane_copy(d) for d in range(1, plane_size)]
    for copy, _ in plane_copies:
        copy.start()
    tangent_sweep(0, steps - 1)
    for _, copy in plane_copies:
        copy.wait_recv()

    def group_sums(k):
        tile = plane[k * space_count]
        for x in range(1, space_count):
            tile = tile + plane[k * space_count + x]
        return jnp.sum(tile, axis=1, keepdims=True)

    def group_terms(k):
        s = group_sums(k)
        norm, gf, fv0, vv0, gv0, fv1, vv1, gv1, pp, ss, flux = [s[r : r + 1] for r in range(11)]
        norm = norm + EPS
        a, b = fv0 / norm, fv1 / norm
        return [pp, vv0 - a * fv0, gv0 - a * gf, ss, vv1 - b * fv1, gv1 - b * gf, flux, b]

    terms = [group_terms(k) for k in range(planes)]
    summed = [sum(t[r] for t in terms[1:]) + terms[0][r] for r in range(7)]
    c1 = group_terms(seg // rows)[7]
    line[line_me] = jnp.concatenate([jnp.broadcast_to(t, (1, 128)) for t in [*summed, c1]], axis=0)

    def line_copy(d):
        j, peer = line_peer(d)
        send = pltpu.make_async_remote_copy(
            src_ref=line.at[line_me], dst_ref=line.at[line_me], send_sem=line_send.at[d],
            recv_sem=line_recv.at[line_me], device_id=peer, device_id_type=MESH,
        )
        receive = pltpu.make_async_remote_copy(
            src_ref=line.at[j], dst_ref=line.at[j], send_sem=line_send.at[d],
            recv_sem=line_recv.at[j], device_id=peer, device_id_type=MESH,
        )
        return send, receive

    line_copies = [line_copy(d) for d in range(1, line_size)]
    to_before = pltpu.make_async_remote_copy(
        src_ref=line.at[line_me], dst_ref=line_next, send_sem=line_send.at[0],
        recv_sem=line_next_sem, device_id=(before, space), device_id_type=MESH,
    )
    to_before.start()
    for copy, _ in line_copies:
        copy.start()
    tangent_sweep(steps - 1, steps)
    for _, copy in line_copies:
        copy.wait_recv()
    to_before.wait_recv()

    whole = line[0]
    for k in range(1, line_size):
        whole = whole + line[k]
    rr, q0, g0, m11, q1, g1, flux = [whole[r : r + 1, 0:1] for r in range(7)]
    c1_next = line_next[7:8, 0:1]
    k0 = rr + q0
    k11 = m11 + q1
    alpha0 = rr / k0
    fresh = alpha0 * alpha0 * m11 - rr
    beta = fresh / rr
    more = 1.0 + beta
    alpha1 = fresh / (more * more * k0 - 2.0 * alpha0 * more * m11 + alpha0 * alpha0 * k11)
    sens = flux + alpha0 * g0 + alpha1 * (more * g0 - alpha0 * g1)
    sens_out[...] = jnp.broadcast_to(sens, sens_out.shape)

    mult_out[...] = (alpha0 + alpha1 * more) * p0[...] - (alpha1 * alpha0) * s1[...]
    arrived(send_w1)
    s2 = 2.0 * s1[...] + state[...] - c1 * tang_flow[...] - w1_next[...] + c1_next * flow_next[...]
    res_out[...] = active * (
        p0[...] - (alpha0 + alpha1 * more) * s1[...] + (alpha1 * alpha0) * s2
    )

    for copies in (send_flow, send_p0, send_w0, send_y0, send_w1):
        for copy in copies:
            copy.wait_send()
    for copy, _ in near_copies + plane_copies + line_copies:
        copy.wait_send()
    to_before.wait_send()


def on_device(rows, axes, advect, growth, forcing, flux_weight, flow_dir, helmholtz):
    steps, height, width = advect.shape[1], advect.shape[3], advect.shape[4]
    seg_count, space_count = axes
    planes = seg_count // rows
    plane_size = planes * space_count
    field = pltpu.VMEM((height, width), F32)
    steps_bf16 = pltpu.VMEM((steps, height, width), BF16)
    half = width // 2
    dma = pltpu.SemaphoreType.DMA
    shape = (steps, height, width)
    mult, res, sens = pl.pallas_call(
        functools.partial(kernel, (seg_count, space_count, rows)),
        out_shape=(
            jax.ShapeDtypeStruct((height, width), F32),
            jax.ShapeDtypeStruct((height, width), F32),
            jax.ShapeDtypeStruct((8, 128), F32),
        ),
        in_specs=[pl.BlockSpec(memory_space=pl.ANY)] * 7,
        out_specs=tuple([pl.BlockSpec(memory_space=pltpu.VMEM)] * 3),
        scratch_shapes=[
            steps_bf16, steps_bf16, steps_bf16, steps_bf16, field,
            pltpu.VMEM((height, height), F32), pltpu.VMEM((4, half, half), BF16),
            pltpu.VMEM((4, height, height), BF16),
            *[field] * 9,
            *[field] * 5,
            pltpu.VMEM((space_count, 8, 128), F32), pltpu.VMEM((space_count, 8, 128), F32),
            pltpu.VMEM((plane_size, 16, 128), F32), pltpu.VMEM((rows, 8, 128), F32), pltpu.VMEM((8, 128), F32),
            dma((3 * steps + 4,)), dma((5, CHUNKS)), dma((5, CHUNKS)),
            dma((2 * space_count - 1,)), dma((space_count,)), dma((space_count,)),
            dma((plane_size,)), dma((plane_size,)), dma((rows,)), dma((rows,)), dma,
        ],
        compiler_params=pltpu.CompilerParams(
            collective_id=0, has_side_effects=True, vmem_limit_bytes=48 << 20
        ),
        cost_estimate=pl.CostEstimate(flops=8_000_000_000, bytes_accessed=6_000_000, transcendentals=0),
    )(
        advect.reshape(shape), growth.reshape(shape), forcing.reshape(shape), flux_weight.reshape(shape),
        flow_dir.reshape(height, width), helmholtz.reshape(height, height),
        jnp.asarray(derivative_tables(width)),
    )
    return mult[None, None], res[None, None], sens[0, 0]


def solution(mesh):
    in_specs = (
        P("seg", None, "space", None, None),
        P("seg", None, "space", None, None),
        P("seg", None, "space", None, None),
        P("seg", None, "space", None, None),
        P("seg", "space", None, None),
        P("space", None, None),
    )
    out_specs = (P("seg", "space", None, None), P("seg", "space", None, None), P())
    axes = (mesh.shape["seg"], mesh.shape["space"])
    rows = 16 if axes[0] % 16 == 0 else axes[0]
    return jax.shard_map(
        functools.partial(on_device, rows, axes), mesh=mesh, in_specs=in_specs, out_specs=out_specs, check_vma=False
    )
```

time: 543 us -> 57.3 us (0.11); the launches traced: 536 us -> 57 us
  blocking collectives: 316 us -> 0 us
  matrix products: 159 us -> 0 us
  Pallas kernels: 0 us -> 47.5 us
  starting transfers between devices: 15.7 us -> 0 us
  between operations: 15.7 us -> 0.65 us
  local copies, waits for them, and re-layouts: 21.6 us -> 8.8 us
  other arithmetic: 7.42 us -> 0 us
    psum x6 -> x0, blocking collectives: 316 us -> none  [the longest x2 151 us: squares(): return lax.psum(jnp.sum(residual * residual), ('seg', 'space'))]
    dot_general x40 -> x0, matrix products: 159 us -> none  [the longest x20 141 us: derive(): return jnp.matmul(field, derivative.T, precision=HIGH)]
    pallas_call x0 -> x1, Pallas kernels: none -> 47.5 us  [on_device(): pl.pallas_call(functools.partial(kernel, (seg_count, space_count, rows)),...]
    ppermute x4 -> x0, starting transfers between devices: 15.7 us -> none  [shifted(): return lax.ppermute(block, axis, route)]
    unnamed x121 -> x14, local copies, waits for them, and re-layouts: 19.3 us -> 8.28 us
  transfers between devices with their start and end apart: 4 -> 0, of which waited for: 0 -> 0; matrix products, arithmetic and copies ran while one was open for 18% -> 0% of each run, Pallas kernels for 0% -> 0%
where the time goes in v1:
time: 57.3 us; the launch traced here: 57 us
  Pallas kernels  47.5 us (83%)
  local copies, waits for them, and re-layouts  8.8 us (15%)
  between operations  0.65 us (1%)
    pallas_call x1, Pallas kernels, on_device(): pl.pallas_call(functools.partial(kernel, (seg_count, space_count, rows)),...  47.5 us
    unnamed x14, local copies, waits for them, and re-layouts  8.28 us

profile of v1, /device:TPU:1, one launch (start us, length us, event | category | flops | bytes accessed | tf_op | source)
XLA Modules:
  0.0 57.0 jit_solution(17254977427705354782)
XLA Ops:
  0.6 0.0 copy-start
  0.6 1.2 %copy-done = bf16[1,4,1,256,512]{4,3,2,1,0:T(8,128)(2,1)S(1)} copy-done((bf16[1,4,1,256,512]{4,3,2,1,0:T(8,128)(2,1)S(1)}, bf16[1,4,1,256,512]{4,3,2,1,0:T(8,128)(2,1)}, u32[]{:S(2)}) %copy-start) | copy-done | bytes 1048600
  1.9 0.0 copy-start.1
  1.9 1.2 %copy-done.1 = bf16[1,4,1,256,512]{4,3,2,1,0:T(8,128)(2,1)S(1)} copy-done((bf16[1,4,1,256,512]{4,3,2,1,0:T(8,128)(2,1)S(1)}, bf16[1,4,1,256,512]{4,3,2,1,0:T(8,128)(2,1)}, u32[]{:S(2)}) %copy-start.1) | copy-done | bytes 1048600
  3.1 0.0 copy-start.2
  3.1 1.2 %copy-done.2 = bf16[1,4,1,256,512]{4,3,2,1,0:T(8,128)(2,1)S(1)} copy-done((bf16[1,4,1,256,512]{4,3,2,1,0:T(8,128)(2,1)S(1)}, bf16[1,4,1,256,512]{4,3,2,1,0:T(8,128)(2,1)}, u32[]{:S(2)}) %copy-start.2) | copy-done | bytes 1048600
  4.3 0.0 copy-start.3
  4.3 1.0 %copy-done.3 = f32[1,1,256,512]{3,2,1,0:T(8,128)S(1)} copy-done((f32[1,1,256,512]{3,2,1,0:T(8,128)S(1)}, f32[1,1,256,512]{3,2,1,0:T(8,128)}, u32[]{:S(2)}) %copy-start.3) | copy-done | bytes 524312
  5.4 0.0 copy-start.4
  5.4 0.9 %copy-done.4 = f32[1,256,256]{2,1,0:T(8,128)S(1)} copy-done((f32[1,256,256]{2,1,0:T(8,128)S(1)}, f32[1,256,256]{2,1,0:T(8,128)}, u32[]{:S(2)}) %copy-start.4) | copy-done | bytes 262168
  6.3 0.0 copy-start.5
  6.3 1.0 %copy-done.5 = bf16[4,256,256]{2,1,0:T(8,128)(2,1)S(1)} copy-done((bf16[4,256,256]{2,1,0:T(8,128)(2,1)S(1)}, bf16[4,256,256]{2,1,0:T(8,128)(2,1)}, u32[]{:S(2)}) %copy-start.5) | copy-done | bytes 524312
  7.3 47.5 %shard_map.94 = (f32[256,512]{1,0:T(8,128)S(1)}, f32[256,512]{1,0:T(8,128)S(1)}, f32[8,128]{1,0:T(8,128)S(1)}) custom-call(bf16[4,256,512]{2,1,0:T(8,128)(2,1)S(1)} %bitcast.11, bf16[4,256,512]{2,1,0:T(8,128)(2,1)S(1)} %bitcast.12, bf16[4,256,512]{2,1,0:T(8,128)(2,1)S(1)} %bitcast.13, bf16[4,256,512]{2,1,0:T(8,128)(2,1)} %bitcast.16, ...), custom_call_target="tpu_custom_call" | custom-call | flops 8000000000 | bytes 6000000 | tf_op jit(solution)/shard_map/pallas_call | solution.py:409
  54.9 0.5 slice.3
  55.4 0.8 %copy.12 = f32[1,1,256,512]{3,2,1,0:T(8,128)} copy(f32[1,1,256,512]{3,2,1,0:T(8,128)S(1)} %bitcast.10) | data formatting | bytes 1048576
  56.2 0.8 %copy.13 = f32[1,1,256,512]{3,2,1,0:T(8,128)} copy(f32[1,1,256,512]{3,2,1,0:T(8,128)S(1)} %bitcast.9) | data formatting | bytes 1048576
Async XLA Ops:
  0.6 1.2 %copy-start = (bf16[1,4,1,256,512]{4,3,2,1,0:T(8,128)(2,1)S(1)}, bf16[1,4,1,256,512]{4,3,2,1,0:T(8,128)(2,1)}, u32[]{:S(2)}) copy-start(bf16[1,4,1,256,512]{4,3,2,1,0:T(8,128)(2,1)} %param.7) | copy-start | bytes 3145732
  1.9 1.2 %copy-start.1 = (bf16[1,4,1,256,512]{4,3,2,1,0:T(8,128)(2,1)S(1)}, bf16[1,4,1,256,512]{4,3,2,1,0:T(8,128)(2,1)}, u32[]{:S(2)}) copy-start(bf16[1,4,1,256,512]{4,3,2,1,0:T(8,128)(2,1)} %param.8) | copy-start | bytes 3145732
  3.1 1.2 %copy-start.2 = (bf16[1,4,1,256,512]{4,3,2,1,0:T(8,128)(2,1)S(1)}, bf16[1,4,1,256,512]{4,3,2,1,0:T(8,128)(2,1)}, u32[]{:S(2)}) copy-start(bf16[1,4,1,256,512]{4,3,2,1,0:T(8,128)(2,1)} %param.9) | copy-start | bytes 3145732
  4.3 1.0 %copy-start.3 = (f32[1,1,256,512]{3,2,1,0:T(8,128)S(1)}, f32[1,1,256,512]{3,2,1,0:T(8,128)}, u32[]{:S(2)}) copy-start(f32[1,1,256,512]{3,2,1,0:T(8,128)} %param.11) | copy-start | bytes 1572868
  5.4 0.9 %copy-start.4 = (f32[1,256,256]{2,1,0:T(8,128)S(1)}, f32[1,256,256]{2,1,0:T(8,128)}, u32[]{:S(2)}) copy-start(f32[1,256,256]{2,1,0:T(8,128)} %param.12) | copy-start | bytes 786436
  6.3 1.0 %copy-start.5 = (bf16[4,256,256]{2,1,0:T(8,128)(2,1)S(1)}, bf16[4,256,256]{2,1,0:T(8,128)(2,1)}, u32[]{:S(2)}) copy-start(bf16[4,256,256]{2,1,0:T(8,128)(2,1)} %constant.2.clone.tables_in) | copy-start | bytes 1572868

commit v2 on v1

--- a/solution.py
+++ b/solution.py
@@ -3,7 +3,6 @@
 
 import jax
 import jax.numpy as jnp
-import numpy as np
 from jax import lax
 from jax.experimental import pallas as pl
 from jax.experimental.pallas import tpu as pltpu
@@ -16,20 +15,33 @@
 CHUNKS = 4
 
 
+def cotangent(angle):
+    square = angle * angle
+    sine = jnp.ones_like(angle)
+    for n in (13, 11, 9, 7, 5, 3):
+        sine = 1.0 - square * sine * (1.0 / (n * (n - 1)))
+    cosine = jnp.ones_like(angle)
+    for n in (14, 12, 10, 8, 6, 4, 2):
+        cosine = 1.0 - square * cosine * (1.0 / (n * (n - 1)))
+    return cosine / (angle * sine)
+
+
 def derivative_tables(width):
-    offset = np.arange(width)
-    angle = np.where(offset == 0, 1, offset) * (math.pi / width)
-    wave = 0.5 * np.where(offset % 2 == 0, 1.0, -1.0) / np.tan(angle) / width
-    wave[0] = 0.0
     half = width // 2
-    index = np.arange(half)
-    apart = index[None, :] - index[:, None]
-    near, far = wave[apart % width], wave[(apart + half) % width]
-    pieces = []
-    for table in (0.5 * (near + far), 0.5 * (near - far)):
-        high = table.astype(np.float32).astype(jnp.bfloat16)
-        pieces += [high, (table - high.astype(np.float64)).astype(np.float32).astype(jnp.bfloat16)]
-    return np.stack(pieces)
+    column = lax.broadcasted_iota(jnp.int32, (8, width), 1)
+    apart = jnp.where(column < half, column, width - column)
+    inside = jnp.logical_and(apart > 0, apart < half)
+    apart = jnp.where(inside, apart, 1)
+    step = math.pi / width
+    near = cotangent(apart.astype(F32) * step)
+    far = cotangent((half - apart).astype(F32) * step)
+    sign = jnp.where((column < half) == (apart % 2 == 0), 0.25 / width, -0.25 / width)
+    sign = jnp.where(inside, sign, 0.0)
+    tables = []
+    for row in (sign * (near - far), sign * (near + far)):
+        block = jnp.concatenate([row] * (half // 8), axis=0)
+        tables.append(pltpu.roll(block, 0, 1, stride=1, stride_axis=0)[:, :half])
+    return tables
 
 
 def dot(a, b):
@@ -66,12 +78,12 @@
 
 
 def kernel(
-    groups, advect_in, growth_in, forcing_in, weight_in, flow_in, helm_in, tables_in,
+    groups, advect_in, growth_in, forcing_in, weight_in, flow_in, helm_in,
     mult_out, res_out, sens_out,
     advect, growth, forcing, weight, flow, helm, tables, matrix,
-    state, p0, w0, y0, s1, w1, tang_flow, grad, v1,
+    state, other, p0, w0, y0, s1, w1, tang_flow, grad,
     flow_next, p_prev, w0_next, y_prev, w1_next,
-    near_own, near_next, plane, line, line_next,
+    near_own, near_next, plane, line, line_next, coef,
     load_sem, send_sem, recv_sem,
     near_send, near_recv, next_recv, plane_send, plane_recv, line_send, line_recv, line_next_sem,
 ):
@@ -86,25 +98,25 @@
     def load(slot, source, target):
         return pltpu.make_async_copy(source, target, load_sem.at[slot])
 
+    def load_forcing(n):
+        return load(n, forcing_in.at[n], forcing.at[n])
+
     def step_loads(n):
         return (
-            load(n, forcing_in.at[n], forcing.at[n]),
             load(steps + n, advect_in.at[n], advect.at[n]),
             load(2 * steps + n, growth_in.at[n], growth.at[n]),
         )
 
     base = 3 * steps
     load_helm = load(base, helm_in, helm)
-    load_tables = load(base + 1, tables_in, tables)
-    load_flow = load(base + 2, flow_in, flow)
-    load_weight = load(base + 3, weight_in, weight)
+    load_flow = load(base + 1, flow_in, flow)
+    load_weight = load(base + 2, weight_in, weight)
     load_helm.start()
-    step_loads(0)[0].start()
-    load_tables.start()
+    load_forcing(0).start()
     for n in range(1, steps):
-        for copy in step_loads(n):
+        for copy in (load_forcing(n), *step_loads(n)):
             copy.start()
-    for copy in step_loads(0)[1:]:
+    for copy in step_loads(0):
         copy.start()
     load_flow.start()
     load_weight.start()
@@ -157,135 +169,178 @@
     send_y0 = transfer(3, y0, y_prev, after)
     send_w1 = transfer(4, w1, w1_next, before)
 
-    def spread(d_table):
-        return [tables[k] for k in range(4)]
-
     def forward():
         return matrix[0], matrix[1]
 
     def backward():
         return matrix[2], matrix[3]
 
-    def tangent_step(n, forced):
-        now = state[...]
+    def tangent(n, now, forced=False):
         rate = growth[n].astype(F32)
         speed = advect[n].astype(F32)
-        update = now + rate * now - speed * derive(now, spread(0))
+        update = now + rate * now - speed * derive(now, [tables[k] for k in range(4)])
         if forced:
             update = update + forcing[n].astype(F32)
-        state[...] = mix(forward(), update)
+        return mix(forward(), update)
 
     def adjoint_rest(n, pulled):
         rate = growth[n].astype(F32)
         speed = advect[n].astype(F32)
-        return pulled + rate * pulled + derive(speed * pulled, spread(0))
+        return pulled + rate * pulled + derive(speed * pulled, [tables[k] for k in range(4)])
 
     def tangent_sweep(first, last):
         @pl.loop(first, last)
         def _(n):
-            tangent_step(n, False)
+            state[...] = tangent(n, state[...])
 
     def adjoint_sweep():
         @pl.loop(0, steps)
         def _(k):
             state[...] = adjoint_rest(steps - 1 - k, mix(backward(), state[...]))
 
+    def gradient_step(k, now, flux):
+        n = steps - 1 - k
+        pulled = mix(backward(), weight[n].astype(F32) + now)
+        return adjoint_rest(n, pulled), flux + lanes(pulled * forcing[n].astype(F32))
+
+    def put(row, value):
+        plane[plane_me, pl.ds(row, 1), :] = value
+
+    for k, table in enumerate(derivative_tables(width)):
+        tables[2 * k], tables[2 * k + 1] = split(table)
+
     load_helm.wait()
     high, low = split(helm[...])
     matrix[0], matrix[1] = high, low
+    load_forcing(0).wait()
+    state[...] = dot(matrix[0], forcing[0]) + dot(matrix[1], forcing[0])
     high, low = split(helm[...].T)
     matrix[2], matrix[3] = high, low
-    step_loads(0)[0].wait()
-    state[...] = dot(matrix[0], forcing[0]) + dot(matrix[1], forcing[0])
     pl.semaphore_wait(barrier, len(greeted))
     start(send_flow)
-    load_tables.wait()
 
     @pl.loop(1, steps)
     def _(n):
-        for copy in step_loads(n):
+        for copy in (load_forcing(n), *step_loads(n)):
             copy.wait()
-        tangent_step(n, True)
-
-    p0[...] = -active * state[...]
-    start(send_p0)
-
-    for copy in step_loads(0)[1:]:
+        state[...] = tangent(n, state[...], forced=True)
+
+    for c in range(CHUNKS):
+        part = pl.ds(c * piece, piece)
+        p0[part, :] = -active * state[part, :]
+        send_p0[c].start()
+
+    for copy in step_loads(0):
         copy.wait()
     state[...] = p0[...]
     adjoint_sweep()
     w0[...] = state[...]
     start(send_w0)
-
     load_flow.wait()
-    state[...] = flow[...]
-    tangent_sweep(0, steps)
-    tang_flow[...] = state[...]
-
     load_weight.wait()
-    state[...] = jnp.zeros_like(state)
-
-    def gradient_step(k, flux):
-        n = steps - 1 - k
-        pulled = mix(backward(), weight[n].astype(F32) + state[...])
-        state[...] = adjoint_rest(n, pulled)
-        return flux + lanes(pulled * forcing[n].astype(F32))
-
-    flux_row = lax.fori_loop(0, steps, gradient_step, jnp.zeros((1, 128), F32))
-    grad[...] = state[...]
-
-    ff_row = lanes(flow[...] * flow[...])
-    gf_row = lanes(grad[...] * flow[...])
-    pp_row = lanes(p0[...] * p0[...])
-
-    arrived(send_p0)
-    state[...] = w0[...] - p_prev[...]
-    fv0_row = lanes(flow[...] * state[...])
-    near_own[space] = jnp.concatenate([ff_row, fv0_row, jnp.zeros((6, 128), F32)], axis=0)
-    near_copies = []
-    for d in range(1, space_count):
-        j = lax.rem(space + d, space_count)
-        near_copies.append(
-            (
-                pltpu.make_async_remote_copy(
-                    src_ref=near_own.at[space], dst_ref=near_own.at[space], send_sem=near_send.at[d - 1],
-                    recv_sem=near_recv.at[space], device_id=(seg, j), device_id_type=MESH,
-                ),
-                pltpu.make_async_remote_copy(
-                    src_ref=near_own.at[j], dst_ref=near_own.at[j], send_sem=near_send.at[d - 1],
-                    recv_sem=near_recv.at[j], device_id=(seg, j), device_id_type=MESH,
-                ),
+    put(0, lanes(flow[...] * flow[...]))
+    put(8, lanes(p0[...] * p0[...]))
+    plane[plane_me, pl.ds(11, 5), :] = jnp.zeros((5, 128), F32)
+
+    def near_pairs():
+        pairs = []
+        for d in range(2 * space_count):
+            own = d < space_count
+            if d == 0:
+                continue
+            j = lax.rem(space + d, space_count)
+            kept, sems = (near_own, near_recv) if own else (near_next, next_recv)
+            to = (seg if own else before, j)
+            pairs.append(
+                (
+                    pltpu.make_async_remote_copy(
+                        src_ref=near_own.at[space], dst_ref=kept.at[space], send_sem=near_send.at[d - 1],
+                        recv_sem=sems.at[space], device_id=to, device_id_type=MESH,
+                    ),
+                    pltpu.make_async_remote_copy(
+                        src_ref=near_own.at[space], dst_ref=kept.at[j], send_sem=near_send.at[d - 1],
+                        recv_sem=sems.at[j], device_id=to, device_id_type=MESH,
+                    ),
+                )
             )
+        return pairs
+
+    near_copies = near_pairs()
+
+    def begin_v0():
+        arrived(send_p0)
+        state[...] = w0[...] - p_prev[...]
+        row = lanes(flow[...] * state[...])
+        put(2, row)
+        near_own[space] = jnp.concatenate(
+            [plane[plane_me, pl.ds(0, 1), :], row, jnp.zeros((6, 128), F32)], axis=0
         )
-    for d in range(space_count):
-        j = lax.rem(space + d, space_count)
-        near_copies.append(
-            (
-                pltpu.make_async_remote_copy(
-                    src_ref=near_own.at[space], dst_ref=near_next.at[space],
-                    send_sem=near_send.at[space_count - 1 + d], recv_sem=next_recv.at[space],
-                    device_id=(before, j), device_id_type=MESH,
-                ),
-                pltpu.make_async_remote_copy(
-                    src_ref=near_own.at[j], dst_ref=near_next.at[j],
-                    send_sem=near_send.at[space_count - 1 + d], recv_sem=next_recv.at[j],
-                    device_id=(before, j), device_id_type=MESH,
-                ),
-            )
-        )
-    for copy, _ in near_copies:
-        copy.start()
-    vv0_row = lanes(state[...] * state[...])
-    gv0_row = lanes(grad[...] * state[...])
-    tangent_sweep(0, steps)
-    for _, copy in near_copies:
-        copy.wait_recv()
-    sums = near_own[0] + near_own[1] + near_own[2] + near_own[3]
-    c0 = total(sums[1:2]) / (total(sums[0:1]) + EPS)
-    sums = near_next[0] + near_next[1] + near_next[2] + near_next[3]
-    c0_next = total(sums[1:2]) / (total(sums[0:1]) + EPS)
-    y0[...] = state[...] - c0 * tang_flow[...]
-    start(send_y0)
+        for copy, _ in near_copies:
+            copy.start()
+        put(3, lanes(state[...] * state[...]))
+
+    def end_y0():
+        for _, copy in near_copies:
+            copy.wait_recv()
+        for row, kept in ((0, near_own), (1, near_next)):
+            sums = kept[0]
+            for x in range(1, space_count):
+                sums = sums + kept[x]
+            c = total(sums[1:2]) / (total(sums[0:1]) + EPS)
+            coef[pl.ds(row, 1), :] = jnp.broadcast_to(c, (1, 128))
+        c0 = coef[0:1, 0:1]
+        for c in range(CHUNKS):
+            part = pl.ds(c * piece, piece)
+            y0[part, :] = state[part, :] - c0 * tang_flow[part, :]
+            send_y0[c].start()
+
+    second = lax.rem(seg, 2) == 1
+
+    @pl.when(second)
+    def _():
+        begin_v0()
+        other[...] = flow[...]
+
+        @pl.loop(0, steps)
+        def _(n):
+            one, two = tangent(n, state[...]), tangent(n, other[...])
+            state[...] = one
+            other[...] = two
+
+        tang_flow[...] = other[...]
+        end_y0()
+        other[...] = jnp.zeros_like(other)
+
+        def body(k, flux):
+            now, flux = gradient_step(k, other[...], flux)
+            other[...] = now
+            return flux
+
+        put(10, lax.fori_loop(0, steps, body, jnp.zeros((1, 128), F32)))
+        grad[...] = other[...]
+
+    @pl.when(jnp.logical_not(second))
+    def _():
+        other[...] = flow[...]
+        state[...] = jnp.zeros_like(state)
+
+        def body(k, flux):
+            one = tangent(k, other[...])
+            now, flux = gradient_step(k, state[...], flux)
+            other[...] = one
+            state[...] = now
+            return flux
+
+        put(10, lax.fori_loop(0, steps, body, jnp.zeros((1, 128), F32)))
+        tang_flow[...] = other[...]
+        grad[...] = state[...]
+        begin_v0()
+        tangent_sweep(0, steps)
+        end_y0()
+
+    put(1, lanes(grad[...] * flow[...]))
+    put(4, lanes(grad[...] * (w0[...] - p_prev[...])))
+    c0, c0_next = coef[0:1, 0:1], coef[1:2, 0:1]
 
     arrived(send_w0)
     arrived(send_flow)
@@ -294,15 +349,12 @@
     adjoint_sweep()
     w1[...] = state[...]
     start(send_w1)
-    ss_row = lanes(s1[...] * s1[...])
+    put(9, lanes(s1[...] * s1[...]))
 
     arrived(send_y0)
     state[...] = w1[...] - not_first * (2.0 * p_prev[...] + y_prev[...] - w0[...] + c0 * flow[...])
-    v1_rows = [lanes(other * state[...]) for other in (flow[...], state[...], grad[...])]
-    plane[plane_me] = jnp.concatenate(
-        [ff_row, gf_row, fv0_row, vv0_row, gv0_row, *v1_rows, pp_row, ss_row, flux_row, jnp.zeros((5, 128), F32)],
-        axis=0,
-    )
+    for row, factor in ((5, flow), (6, state), (7, grad)):
+        put(row, lanes(factor[...] * state[...]))
 
     def plane_copy(d):
         j, peer = plane_peer(d)
@@ -413,7 +465,7 @@
             jax.ShapeDtypeStruct((height, width), F32),
             jax.ShapeDtypeStruct((8, 128), F32),
         ),
-        in_specs=[pl.BlockSpec(memory_space=pl.ANY)] * 7,
+        in_specs=[pl.BlockSpec(memory_space=pl.ANY)] * 6,
         out_specs=tuple([pl.BlockSpec(memory_space=pltpu.VMEM)] * 3),
         scratch_shapes=[
             steps_bf16, steps_bf16, steps_bf16, steps_bf16, field,
@@ -422,19 +474,18 @@
             *[field] * 9,
             *[field] * 5,
             pltpu.VMEM((space_count, 8, 128), F32), pltpu.VMEM((space_count, 8, 128), F32),
-            pltpu.VMEM((plane_size, 16, 128), F32), pltpu.VMEM((rows, 8, 128), F32), pltpu.VMEM((8, 128), F32),
-            dma((3 * steps + 4,)), dma((5, CHUNKS)), dma((5, CHUNKS)),
+            pltpu.VMEM((plane_size, 16, 128), F32), pltpu.VMEM((rows, 8, 128), F32), pltpu.VMEM((8, 128), F32), pltpu.VMEM((8, 128), F32),
+            dma((3 * steps + 3,)), dma((5, CHUNKS)), dma((5, CHUNKS)),
             dma((2 * space_count - 1,)), dma((space_count,)), dma((space_count,)),
             dma((plane_size,)), dma((plane_size,)), dma((rows,)), dma((rows,)), dma,
         ],
         compiler_params=pltpu.CompilerParams(
-            collective_id=0, has_side_effects=True, vmem_limit_bytes=48 << 20
+            collective_id=0, has_side_effects=True, vmem_limit_bytes=60 << 20
         ),
         cost_estimate=pl.CostEstimate(flops=8_000_000_000, bytes_accessed=6_000_000, transcendentals=0),
     )(
         advect.reshape(shape), growth.reshape(shape), forcing.reshape(shape), flux_weight.reshape(shape),
         flow_dir.reshape(height, width), helmholtz.reshape(height, height),
-        jnp.asarray(derivative_tables(width)),
     )
     return mult[None, None], res[None, None], sens[0, 0]
 

time: 57.3 us -> 53 us (0.925)
  local copies, waits for them, and re-layouts: 8.8 us -> 3.91 us
  Pallas kernels: 47.5 us -> 48.3 us
    unnamed x14 -> x4, local copies, waits for them, and re-layouts: 8.28 us -> 2.72 us
    pallas_call x1, Pallas kernels: 47.5 us -> 48.3 us  [on_device(): pl.pallas_call(functools.partial(kernel, (seg_count, space_count, rows)),...]
    slice x1, local copies, waits for them, and re-layouts: 0.51 us -> 1.18 us  [on_device(): return (mult[None, None], res[None, None], sens[0, 0])]
where the time goes in v2:
time: 53 us; the launch traced here: 52.9 us
  Pallas kernels  48.3 us (91%)
  local copies, waits for them, and re-layouts  3.91 us (7%)
  between operations  0.64 us (1%)
    pallas_call x1, Pallas kernels, on_device(): pl.pallas_call(functools.partial(kernel, (seg_count, space_count, rows)),...  48.3 us
    unnamed x4, local copies, waits for them, and re-layouts  2.72 us
    slice x1, local copies, waits for them, and re-layouts, on_device(): return (mult[None, None], res[None, None], sens[0, 0])  1.18 us

profile of v2, /device:TPU:1, one launch (start us, length us, event | category | flops | bytes accessed | tf_op | source)
XLA Modules:
  0.0 52.9 jit_solution(13910641615331447581)
XLA Ops:
  0.6 48.3 %shard_map.85 = (f32[256,512]{1,0:T(8,128)}, f32[256,512]{1,0:T(8,128)}, f32[8,128]{1,0:T(8,128)}) custom-call(bf16[4,256,512]{2,1,0:T(8,128)(2,1)} %bitcast.11, bf16[4,256,512]{2,1,0:T(8,128)(2,1)} %bitcast.12, bf16[4,256,512]{2,1,0:T(8,128)(2,1)} %bitcast.13, bf16[4,256,512]{2,1,0:T(8,128)(2,1)} %bitcast.14, f32[256,512]{1,0:T(8,128)} %bitcast.15, ...), custom_call_target="tpu_custom_call" | custom-call | flops 8000000000 | bytes 6000000 | tf_op jit(solution)/shard_map/pallas_call | solution.py:461
  49.0 1.2 %slice.3 = f32[1,1]{1,0:T(1,128)} slice(f32[8,128]{1,0:T(8,128)} %get-tuple-element.8), slice={[0:1], [0:1]} | slice | bytes 8 | tf_op jit(solution)/shard_map/slice | solution.py:490
  50.1 0.0 copy-start
  50.1 1.9 %copy.11 = f32[1,1,256,512]{3,2,1,0:T(8,128)} copy(f32[1,1,256,512]{3,2,1,0:T(8,128)} %bitcast.10) | data formatting | bytes 1048576
  52.1 0.0 copy-done
  52.1 0.8 %copy.12 = f32[1,1,256,512]{3,2,1,0:T(8,128)} copy(f32[1,1,256,512]{3,2,1,0:T(8,128)S(1)} %bitcast.9) | data formatting | bytes 1048576
Async XLA Ops:
  50.1 1.9 %copy-start = (f32[256,512]{1,0:T(8,128)S(1)}, f32[256,512]{1,0:T(8,128)}, u32[]{:S(2)}) copy-start(f32[256,512]{1,0:T(8,128)} %get-tuple-element.7) | copy-start | bytes 1572868

commit v3 on v2

--- a/solution.py
+++ b/solution.py
@@ -267,6 +267,13 @@
 
     near_copies = near_pairs()
 
+    def near_ratio(row, kept):
+        sums = kept[0]
+        for x in range(1, space_count):
+            sums = sums + kept[x]
+        c = total(sums[1:2]) / (total(sums[0:1]) + EPS)
+        coef[pl.ds(row, 1), :] = jnp.broadcast_to(c, (1, 128))
+
     def begin_v0():
         arrived(send_p0)
         state[...] = w0[...] - p_prev[...]
@@ -280,14 +287,9 @@
         put(3, lanes(state[...] * state[...]))
 
     def end_y0():
-        for _, copy in near_copies:
+        for _, copy in near_copies[: space_count - 1]:
             copy.wait_recv()
-        for row, kept in ((0, near_own), (1, near_next)):
-            sums = kept[0]
-            for x in range(1, space_count):
-                sums = sums + kept[x]
-            c = total(sums[1:2]) / (total(sums[0:1]) + EPS)
-            coef[pl.ds(row, 1), :] = jnp.broadcast_to(c, (1, 128))
+        near_ratio(0, near_own)
         c0 = coef[0:1, 0:1]
         for c in range(CHUNKS):
             part = pl.ds(c * piece, piece)
@@ -340,10 +342,13 @@
 
     put(1, lanes(grad[...] * flow[...]))
     put(4, lanes(grad[...] * (w0[...] - p_prev[...])))
+
+    for _, copy in near_copies[space_count - 1 :]:
+        copy.wait_recv()
+    near_ratio(1, near_next)
     c0, c0_next = coef[0:1, 0:1], coef[1:2, 0:1]
-
+    arrived(send_flow)
     arrived(send_w0)
-    arrived(send_flow)
     s1[...] = active * (2.0 * p0[...] + y0[...] - w0_next[...] + c0_next * flow_next[...])
     state[...] = s1[...]
     adjoint_sweep()
@@ -448,6 +453,18 @@
     to_before.wait_send()
 
 
+def hand_over(mult_in, res_in, sens_in, mult_out, res_out, sens_out, sems):
+    copies = [
+        pltpu.make_async_copy(mult_in, mult_out, sems.at[0]),
+        pltpu.make_async_copy(res_in, res_out, sems.at[1]),
+    ]
+    for copy in copies:
+        copy.start()
+    sens_out[...] = sens_in[0:1, 0:1]
+    for copy in copies:
+        copy.wait()
+
+
 def on_device(rows, axes, advect, growth, forcing, flux_weight, flow_dir, helmholtz):
     steps, height, width = advect.shape[1], advect.shape[3], advect.shape[4]
     seg_count, space_count = axes
@@ -458,12 +475,12 @@
     half = width // 2
     dma = pltpu.SemaphoreType.DMA
     shape = (steps, height, width)
-    mult, res, sens = pl.pallas_call(
+    results = pl.pallas_call(
         functools.partial(kernel, (seg_count, space_count, rows)),
         out_shape=(
-            jax.ShapeDtypeStruct((height, width), F32),
-            jax.ShapeDtypeStruct((height, width), F32),
-            jax.ShapeDtypeStruct((8, 128), F32),
+            pltpu.VMEM((height, width), F32),
+            pltpu.VMEM((height, width), F32),
+            pltpu.VMEM((8, 128), F32),
         ),
         in_specs=[pl.BlockSpec(memory_space=pl.ANY)] * 6,
         out_specs=tuple([pl.BlockSpec(memory_space=pltpu.VMEM)] * 3),
@@ -487,7 +504,19 @@
         advect.reshape(shape), growth.reshape(shape), forcing.reshape(shape), flux_weight.reshape(shape),
         flow_dir.reshape(height, width), helmholtz.reshape(height, height),
     )
-    return mult[None, None], res[None, None], sens[0, 0]
+    mult, res, sens = pl.pallas_call(
+        hand_over,
+        out_shape=(
+            jax.ShapeDtypeStruct((height, width), F32),
+            jax.ShapeDtypeStruct((height, width), F32),
+            jax.ShapeDtypeStruct((1, 1), F32),
+        ),
+        in_specs=[pl.BlockSpec(memory_space=pl.ANY)] * 2 + [pl.BlockSpec(memory_space=pltpu.VMEM)],
+        out_specs=(pl.BlockSpec(memory_space=pl.ANY),) * 2 + (pl.BlockSpec(memory_space=pltpu.VMEM),),
+        scratch_shapes=[dma((2,))],
+        compiler_params=pltpu.CompilerParams(vmem_limit_bytes=1 << 20),
+    )(*results)
+    return mult[None, None], res[None, None], sens.reshape(())
 
 
 def solution(mesh):

time: 53 us -> 45.3 us (0.85)
  local copies, waits for them, and re-layouts: 3.91 us -> 0 us
  Pallas kernels: 48.3 us -> 44.6 us
    pallas_call x1, Pallas kernels: 48.3 us -> 43.1 us  [on_device(): pl.pallas_call(functools.partial(kernel, (seg_count, space_count, rows)),...]
    unnamed x4 -> x0, local copies, waits for them, and re-layouts: 2.72 us -> none
    pallas_call x0 -> x1, Pallas kernels: none -> 1.49 us  [on_device(): pl.pallas_call(hand_over, out_shape=(jax.ShapeDtypeStruct((height, width)...]
    slice x1 -> x0, local copies, waits for them, and re-layouts: 1.18 us -> none  [on_device(): return (mult[None, None], res[None, None], sens[0, 0])]
where the time goes in v3:
time: 45.3 us; the launch traced here: 45.2 us
  Pallas kernels  44.6 us (98%)
  between operations  0.64 us (1%)
    pallas_call x1, Pallas kernels, on_device(): pl.pallas_call(functools.partial(kernel, (seg_count, space_count, rows)),...  43.1 us
    pallas_call x1, Pallas kernels, on_device(): pl.pallas_call(hand_over, out_shape=(jax.ShapeDtypeStruct((height, width)...  1.49 us

profile of v3, /device:TPU:1, one launch (start us, length us, event | category | flops | bytes accessed | tf_op | source)
XLA Modules:
  0.0 45.2 jit_solution(13294863676955583224)
XLA Ops:
  0.6 43.1 %shard_map.85 = (f32[256,512]{1,0:T(8,128)S(1)}, f32[256,512]{1,0:T(8,128)S(1)}, f32[8,128]{1,0:T(8,128)S(1)}) custom-call(bf16[4,256,512]{2,1,0:T(8,128)(2,1)} %bitcast.9, bf16[4,256,512]{2,1,0:T(8,128)(2,1)} %bitcast.10, bf16[4,256,512]{2,1,0:T(8,128)(2,1)} %bitcast.11, bf16[4,256,512]{2,1,0:T(8,128)(2,1)} %bitcast.12, f32[256,512]{1,0:T(8,128)} %bitcast.13, ...), custom_call_target="tpu_custom_call" | custom-call | flops 8000000000 | bytes 6000000 | tf_op jit(solution)/shard_map/pallas_call | solution.py:478
  43.7 1.5 %shard_map.86 = (f32[256,512]{1,0:T(8,128)}, f32[256,512]{1,0:T(8,128)}, f32[1,1]{1,0:T(1,128)}) custom-call(f32[256,512]{1,0:T(8,128)S(1)} %get-tuple-element.9.mult_in, f32[256,512]{1,0:T(8,128)S(1)} %get-tuple-element.10.res_in, f32[8,128]{1,0:T(8,128)S(1)} %get-tuple-element.11.sens_in), custom_call_target="tpu_custom_call" | custom-call | tf_op jit(solution)/shard_map/pallas_call | solution.py:507

commit v4 on v3

--- a/solution.py
+++ b/solution.py
@@ -80,8 +80,8 @@
 def kernel(
     groups, advect_in, growth_in, forcing_in, weight_in, flow_in, helm_in,
     mult_out, res_out, sens_out,
-    advect, growth, forcing, weight, flow, helm, tables, matrix,
-    state, other, p0, w0, y0, s1, w1, tang_flow, grad,
+    advect, growth, forcing, weight, helm, tables, matrix,
+    from_p0, from_s1, from_flow, from_v, from_weight, y0,
     flow_next, p_prev, w0_next, y_prev, w1_next,
     near_own, near_next, plane, line, line_next, coef,
     load_sem, send_sem, recv_sem,
@@ -106,6 +106,11 @@
             load(steps + n, advect_in.at[n], advect.at[n]),
             load(2 * steps + n, growth_in.at[n], growth.at[n]),
         )
+
+    p0, w0 = from_p0.at[0], from_p0.at[steps]
+    s1, w1 = from_s1.at[0], from_s1.at[steps]
+    flow, grad = from_flow.at[0], from_weight.at[steps]
+    v = from_v.at[0]
 
     base = 3 * steps
     load_helm = load(base, helm_in, helm)
@@ -125,17 +130,29 @@
     line_me = lax.rem(seg, rows)
     plane_size, line_size = planes * space_count, rows
 
-    def plane_peer(d):
-        j = lax.rem(plane_me + d, plane_size)
-        return j, (lax.div(j, space_count) * rows + line_me, lax.rem(j, space_count))
-
-    def line_peer(d):
-        j = lax.rem(line_me + d, line_size)
-        return j, ((seg // rows) * rows + j, space)
+    def ring(distance, size):
+        return min(distance, size - distance)
+
+    def offsets(first, second):
+        pairs = [(a, b) for a in range(first) for b in range(second)][1:]
+        return sorted(pairs, key=lambda pair: -ring(pair[0], first) - ring(pair[1], second))
+
+    plane_shifts = offsets(planes, space_count)
+    line_shifts = offsets(rows // 2, 2)
+
+    def plane_peer(shift):
+        plane_at = lax.rem(lax.div(seg, rows) + shift[0], planes)
+        x = lax.rem(space + shift[1], space_count)
+        return plane_at * space_count + x, (plane_at * rows + line_me, x)
+
+    def line_peer(shift):
+        chip = lax.rem(lax.div(line_me, 2) + shift[0], rows // 2)
+        j = chip * 2 + lax.rem(lax.rem(line_me, 2) + shift[1], 2)
+        return j, (lax.div(seg, rows) * rows + j, space)
 
     barrier = pltpu.get_barrier_semaphore()
-    greeted = [plane_peer(d)[1] for d in range(1, plane_size)]
-    greeted += [line_peer(d)[1] for d in range(1, line_size)]
+    greeted = [plane_peer(shift)[1] for shift in plane_shifts]
+    greeted += [line_peer(shift)[1] for shift in line_shifts]
     greeted += [(s, lax.rem(space + d, space_count)) for s in (before, after) for d in range(space_count)]
     for peer in greeted:
         pl.semaphore_signal(barrier, inc=1, device_id=peer, device_id_type=MESH)
@@ -155,6 +172,8 @@
             for c in range(CHUNKS)
         ]
 
+    parts = [pl.ds(c * piece, piece) for c in range(CHUNKS)]
+
     def start(copies):
         for copy in copies:
             copy.start()
@@ -188,19 +207,19 @@
         speed = advect[n].astype(F32)
         return pulled + rate * pulled + derive(speed * pulled, [tables[k] for k in range(4)])
 
-    def tangent_sweep(first, last):
+    def tangent_sweep(path, first, last):
         @pl.loop(first, last)
         def _(n):
-            state[...] = tangent(n, state[...])
-
-    def adjoint_sweep():
+            path[n + 1] = tangent(n, path[n])
+
+    def adjoint_sweep(path):
         @pl.loop(0, steps)
         def _(k):
-            state[...] = adjoint_rest(steps - 1 - k, mix(backward(), state[...]))
-
-    def gradient_step(k, now, flux):
+            path[k + 1] = adjoint_rest(steps - 1 - k, mix(backward(), path[k]))
+
+    def gradient_step(k, flux):
         n = steps - 1 - k
-        pulled = mix(backward(), weight[n].astype(F32) + now)
+        pulled = mix(backward(), weight[n].astype(F32) + from_weight[k])
         return adjoint_rest(n, pulled), flux + lanes(pulled * forcing[n].astype(F32))
 
     def put(row, value):
@@ -213,7 +232,7 @@
     high, low = split(helm[...])
     matrix[0], matrix[1] = high, low
     load_forcing(0).wait()
-    state[...] = dot(matrix[0], forcing[0]) + dot(matrix[1], forcing[0])
+    from_v[1] = dot(matrix[0], forcing[0]) + dot(matrix[1], forcing[0])
     high, low = split(helm[...].T)
     matrix[2], matrix[3] = high, low
     pl.semaphore_wait(barrier, len(greeted))
@@ -223,31 +242,27 @@
     def _(n):
         for copy in (load_forcing(n), *step_loads(n)):
             copy.wait()
-        state[...] = tangent(n, state[...], forced=True)
-
-    for c in range(CHUNKS):
-        part = pl.ds(c * piece, piece)
-        p0[part, :] = -active * state[part, :]
-        send_p0[c].start()
+        from_v[n + 1] = tangent(n, from_v[n], forced=True)
+
+    for part, copy in zip(parts, send_p0):
+        p0[part, :] = -active * from_v[steps, part, :]
+        copy.start()
 
     for copy in step_loads(0):
         copy.wait()
-    state[...] = p0[...]
-    adjoint_sweep()
-    w0[...] = state[...]
+    adjoint_sweep(from_p0)
     start(send_w0)
     load_flow.wait()
     load_weight.wait()
+    from_weight[0] = jnp.zeros_like(from_weight[0])
     put(0, lanes(flow[...] * flow[...]))
     put(8, lanes(p0[...] * p0[...]))
     plane[plane_me, pl.ds(11, 5), :] = jnp.zeros((5, 128), F32)
 
     def near_pairs():
         pairs = []
-        for d in range(2 * space_count):
+        for d in range(1, 2 * space_count):
             own = d < space_count
-            if d == 0:
-                continue
             j = lax.rem(space + d, space_count)
             kept, sems = (near_own, near_recv) if own else (near_next, next_recv)
             to = (seg if own else before, j)
@@ -275,94 +290,98 @@
         coef[pl.ds(row, 1), :] = jnp.broadcast_to(c, (1, 128))
 
     def begin_v0():
-        arrived(send_p0)
-        state[...] = w0[...] - p_prev[...]
-        row = lanes(flow[...] * state[...])
+        row = jnp.zeros((1, 128), F32)
+        for part, copy in zip(parts, send_p0):
+            copy.wait_recv()
+            piece_of = w0[part, :] - p_prev[part, :]
+            v[part, :] = piece_of
+            row = row + lanes(flow[part, :] * piece_of)
         put(2, row)
         near_own[space] = jnp.concatenate(
             [plane[plane_me, pl.ds(0, 1), :], row, jnp.zeros((6, 128), F32)], axis=0
         )
         for copy, _ in near_copies:
             copy.start()
-        put(3, lanes(state[...] * state[...]))
-
-    def end_y0():
+        put(3, lanes(v[...] * v[...]))
+
+    def own_ratio():
         for _, copy in near_copies[: space_count - 1]:
             copy.wait_recv()
         near_ratio(0, near_own)
-        c0 = coef[0:1, 0:1]
-        for c in range(CHUNKS):
-            part = pl.ds(c * piece, piece)
-            y0[part, :] = state[part, :] - c0 * tang_flow[part, :]
-            send_y0[c].start()
+        return coef[0:1, 0:1]
 
     second = lax.rem(seg, 2) == 1
 
     @pl.when(second)
     def _():
         begin_v0()
-        other[...] = flow[...]
-
-        @pl.loop(0, steps)
+
+        @pl.loop(0, steps - 1)
         def _(n):
-            one, two = tangent(n, state[...]), tangent(n, other[...])
-            state[...] = one
-            other[...] = two
-
-        tang_flow[...] = other[...]
-        end_y0()
-        other[...] = jnp.zeros_like(other)
+            one, two = tangent(n, from_v[n]), tangent(n, from_flow[n])
+            from_v[n + 1] = one
+            from_flow[n + 1] = two
+
+        y0[...] = tangent(steps - 1, from_v[steps - 1] - own_ratio() * from_flow[steps - 1])
+        start(send_y0)
 
         def body(k, flux):
-            now, flux = gradient_step(k, other[...], flux)
-            other[...] = now
+            now, flux = gradient_step(k, flux)
+            from_weight[k + 1] = now
             return flux
 
         put(10, lax.fori_loop(0, steps, body, jnp.zeros((1, 128), F32)))
-        grad[...] = other[...]
 
     @pl.when(jnp.logical_not(second))
     def _():
-        other[...] = flow[...]
-        state[...] = jnp.zeros_like(state)
-
         def body(k, flux):
-            one = tangent(k, other[...])
-            now, flux = gradient_step(k, state[...], flux)
-            other[...] = one
-            state[...] = now
+            one = tangent(k, from_flow[k])
+            now, flux = gradient_step(k, flux)
+            from_flow[k + 1] = one
+            from_weight[k + 1] = now
             return flux
 
         put(10, lax.fori_loop(0, steps, body, jnp.zeros((1, 128), F32)))
-        tang_flow[...] = other[...]
-        grad[...] = state[...]
         begin_v0()
-        tangent_sweep(0, steps)
-        end_y0()
+        tangent_sweep(from_v, 0, steps)
+        c0 = own_ratio()
+        for part, copy in zip(parts, send_y0):
+            y0[part, :] = from_v[steps, part, :] - c0 * from_flow[steps, part, :]
+            copy.start()
 
     put(1, lanes(grad[...] * flow[...]))
-    put(4, lanes(grad[...] * (w0[...] - p_prev[...])))
+    put(4, lanes(grad[...] * v[...]))
 
     for _, copy in near_copies[space_count - 1 :]:
         copy.wait_recv()
     near_ratio(1, near_next)
     c0, c0_next = coef[0:1, 0:1], coef[1:2, 0:1]
     arrived(send_flow)
-    arrived(send_w0)
-    s1[...] = active * (2.0 * p0[...] + y0[...] - w0_next[...] + c0_next * flow_next[...])
-    state[...] = s1[...]
-    adjoint_sweep()
-    w1[...] = state[...]
+    row = jnp.zeros((1, 128), F32)
+    for part, copy in zip(parts, send_w0):
+        copy.wait_recv()
+        piece_of = active * (
+            2.0 * p0[part, :] + y0[part, :] - w0_next[part, :] + c0_next * flow_next[part, :]
+        )
+        s1[part, :] = piece_of
+        row = row + lanes(piece_of * piece_of)
+    put(9, row)
+    adjoint_sweep(from_s1)
     start(send_w1)
-    put(9, lanes(s1[...] * s1[...]))
-
-    arrived(send_y0)
-    state[...] = w1[...] - not_first * (2.0 * p_prev[...] + y_prev[...] - w0[...] + c0 * flow[...])
-    for row, factor in ((5, flow), (6, state), (7, grad)):
-        put(row, lanes(factor[...] * state[...]))
-
-    def plane_copy(d):
-        j, peer = plane_peer(d)
+
+    v1_rows = [jnp.zeros((1, 128), F32)] * 3
+    for part, copy in zip(parts, send_y0):
+        copy.wait_recv()
+        piece_of = w1[part, :] - not_first * (
+            2.0 * p_prev[part, :] + y_prev[part, :] - w0[part, :] + c0 * flow[part, :]
+        )
+        v[part, :] = piece_of
+        factors = (flow[part, :], piece_of, grad[part, :])
+        v1_rows = [row + lanes(factor * piece_of) for row, factor in zip(v1_rows, factors)]
+    plane[plane_me, pl.ds(5, 3), :] = jnp.concatenate(v1_rows, axis=0)
+
+    def plane_copy(d, shift):
+        j, peer = plane_peer(shift)
         send = pltpu.make_async_remote_copy(
             src_ref=plane.at[plane_me], dst_ref=plane.at[plane_me], send_sem=plane_send.at[d],
             recv_sem=plane_recv.at[plane_me], device_id=peer, device_id_type=MESH,
@@ -373,33 +392,30 @@
         )
         return send, receive
 
-    plane_copies = [plane_copy(d) for d in range(1, plane_size)]
+    plane_copies = [plane_copy(d, shift) for d, shift in enumerate(plane_shifts)]
     for copy, _ in plane_copies:
         copy.start()
-    tangent_sweep(0, steps - 1)
+    tangent_sweep(from_v, 0, steps - 1)
     for _, copy in plane_copies:
         copy.wait_recv()
 
-    def group_sums(k):
+    lane = lax.broadcasted_iota(jnp.int32, (16, 128), 1)
+    sums = jnp.zeros((16, 128), F32)
+    for k in range(planes):
         tile = plane[k * space_count]
         for x in range(1, space_count):
             tile = tile + plane[k * space_count + x]
-        return jnp.sum(tile, axis=1, keepdims=True)
-
-    def group_terms(k):
-        s = group_sums(k)
-        norm, gf, fv0, vv0, gv0, fv1, vv1, gv1, pp, ss, flux = [s[r : r + 1] for r in range(11)]
-        norm = norm + EPS
-        a, b = fv0 / norm, fv1 / norm
-        return [pp, vv0 - a * fv0, gv0 - a * gf, ss, vv1 - b * fv1, gv1 - b * gf, flux, b]
-
-    terms = [group_terms(k) for k in range(planes)]
-    summed = [sum(t[r] for t in terms[1:]) + terms[0][r] for r in range(7)]
-    c1 = group_terms(seg // rows)[7]
-    line[line_me] = jnp.concatenate([jnp.broadcast_to(t, (1, 128)) for t in [*summed, c1]], axis=0)
-
-    def line_copy(d):
-        j, peer = line_peer(d)
+        sums = jnp.where(lane == k, jnp.sum(tile, axis=1, keepdims=True), sums)
+    norm, gf, fv0, vv0, gv0, fv1, vv1, gv1, pp, ss, flux = [sums[r : r + 1] for r in range(11)]
+    norm = norm + EPS
+    a, b = fv0 / norm, fv1 / norm
+    mine = jnp.where(lane[0:1] == lax.div(seg, rows), b, 0.0)
+    line[line_me] = jnp.concatenate(
+        [pp, vv0 - a * fv0, gv0 - a * gf, ss, vv1 - b * fv1, gv1 - b * gf, flux, mine], axis=0
+    )
+
+    def line_copy(d, shift):
+        j, peer = line_peer(shift)
         send = pltpu.make_async_remote_copy(
             src_ref=line.at[line_me], dst_ref=line.at[line_me], send_sem=line_send.at[d],
             recv_sem=line_recv.at[line_me], device_id=peer, device_id_type=MESH,
@@ -410,7 +426,7 @@
         )
         return send, receive
 
-    line_copies = [line_copy(d) for d in range(1, line_size)]
+    line_copies = [line_copy(d + 1, shift) for d, shift in enumerate(line_shifts)]
     to_before = pltpu.make_async_remote_copy(
         src_ref=line.at[line_me], dst_ref=line_next, send_sem=line_send.at[0],
         recv_sem=line_next_sem, device_id=(before, space), device_id_type=MESH,
@@ -418,16 +434,18 @@
     to_before.start()
     for copy, _ in line_copies:
         copy.start()
-    tangent_sweep(steps - 1, steps)
+    c1 = total(mine)
+    from_v[steps] = tangent(steps - 1, from_v[steps - 1] - c1 * from_flow[steps - 1])
+    to_before.wait_recv()
+    c1_next = total(line_next[7:8])
     for _, copy in line_copies:
         copy.wait_recv()
-    to_before.wait_recv()
 
     whole = line[0]
     for k in range(1, line_size):
         whole = whole + line[k]
-    rr, q0, g0, m11, q1, g1, flux = [whole[r : r + 1, 0:1] for r in range(7)]
-    c1_next = line_next[7:8, 0:1]
+    whole = jnp.sum(whole, axis=1, keepdims=True)
+    rr, q0, g0, m11, q1, g1, flux = [whole[r : r + 1] for r in range(7)]
     k0 = rr + q0
     k11 = m11 + q1
     alpha0 = rr / k0
@@ -438,12 +456,12 @@
     sens = flux + alpha0 * g0 + alpha1 * (more * g0 - alpha0 * g1)
     sens_out[...] = jnp.broadcast_to(sens, sens_out.shape)
 
-    mult_out[...] = (alpha0 + alpha1 * more) * p0[...] - (alpha1 * alpha0) * s1[...]
-    arrived(send_w1)
-    s2 = 2.0 * s1[...] + state[...] - c1 * tang_flow[...] - w1_next[...] + c1_next * flow_next[...]
-    res_out[...] = active * (
-        p0[...] - (alpha0 + alpha1 * more) * s1[...] + (alpha1 * alpha0) * s2
-    )
+    along, across = alpha0 + alpha1 * more, alpha1 * alpha0
+    mult_out[...] = along * p0[...] - across * s1[...]
+    for part, copy in zip(parts, send_w1):
+        copy.wait_recv()
+        s2 = 2.0 * s1[part, :] + from_v[steps, part, :] - w1_next[part, :] + c1_next * flow_next[part, :]
+        res_out[part, :] = active * (p0[part, :] - along * s1[part, :] + across * s2)
 
     for copies in (send_flow, send_p0, send_w0, send_y0, send_w1):
         for copy in copies:
@@ -485,10 +503,10 @@
         in_specs=[pl.BlockSpec(memory_space=pl.ANY)] * 6,
         out_specs=tuple([pl.BlockSpec(memory_space=pltpu.VMEM)] * 3),
         scratch_shapes=[
-            steps_bf16, steps_bf16, steps_bf16, steps_bf16, field,
+            steps_bf16, steps_bf16, steps_bf16, steps_bf16,
             pltpu.VMEM((height, height), F32), pltpu.VMEM((4, half, half), BF16),
             pltpu.VMEM((4, height, height), BF16),
-            *[field] * 9,
+            *[pltpu.VMEM((steps + 1, height, width), F32)] * 5, field,
             *[field] * 5,
             pltpu.VMEM((space_count, 8, 128), F32), pltpu.VMEM((space_count, 8, 128), F32),
             pltpu.VMEM((plane_size, 16, 128), F32), pltpu.VMEM((rows, 8, 128), F32), pltpu.VMEM((8, 128), F32), pltpu.VMEM((8, 128), F32),

time: 45.3 us -> 43.8 us (0.967)
  Pallas kernels: 44.6 us -> 43.1 us
    pallas_call x1, Pallas kernels: 43.1 us -> 41.6 us  [on_device(): pl.pallas_call(functools.partial(kernel, (seg_count, space_count, rows)),...]
where the time goes in v4:
time: 43.8 us; the launch traced here: 43.7 us
  Pallas kernels  43.1 us (98%)
  between operations  0.64 us (1%)
    pallas_call x1, Pallas kernels, on_device(): pl.pallas_call(functools.partial(kernel, (seg_count, space_count, rows)),...  41.6 us
    pallas_call x1, Pallas kernels, on_device(): pl.pallas_call(hand_over, out_shape=(jax.ShapeDtypeStruct((height, width)...  1.49 us

profile of v4, /device:TPU:1, one launch (start us, length us, event | category | flops | bytes accessed | tf_op | source)
XLA Modules:
  0.0 43.7 jit_solution(2416516935908865907)
XLA Ops:
  0.6 41.6 %shard_map.85 = (f32[256,512]{1,0:T(8,128)S(1)}, f32[256,512]{1,0:T(8,128)S(1)}, f32[8,128]{1,0:T(8,128)S(1)}) custom-call(bf16[4,256,512]{2,1,0:T(8,128)(2,1)} %bitcast.9, bf16[4,256,512]{2,1,0:T(8,128)(2,1)} %bitcast.10, bf16[4,256,512]{2,1,0:T(8,128)(2,1)} %bitcast.11, bf16[4,256,512]{2,1,0:T(8,128)(2,1)} %bitcast.12, f32[256,512]{1,0:T(8,128)} %bitcast.13, ...), custom_call_target="tpu_custom_call" | custom-call | flops 8000000000 | bytes 6000000 | tf_op jit(solution)/shard_map/pallas_call | solution.py:496
  42.2 1.5 %shard_map.86 = (f32[256,512]{1,0:T(8,128)}, f32[256,512]{1,0:T(8,128)}, f32[1,1]{1,0:T(1,128)}) custom-call(f32[256,512]{1,0:T(8,128)S(1)} %get-tuple-element.9.mult_in, f32[256,512]{1,0:T(8,128)S(1)} %get-tuple-element.10.res_in, f32[8,128]{1,0:T(8,128)S(1)} %get-tuple-element.11.sens_in), custom_call_target="tpu_custom_call" | custom-call | tf_op jit(solution)/shard_map/pallas_call | solution.py:525

commit v5 on v4

--- a/solution.py
+++ b/solution.py
@@ -79,7 +79,7 @@
 
 def kernel(
     groups, advect_in, growth_in, forcing_in, weight_in, flow_in, helm_in,
-    mult_out, res_out, sens_out,
+    p0_out, s1_out, s2_out, coef_out,
     advect, growth, forcing, weight, helm, tables, matrix,
     from_p0, from_s1, from_flow, from_v, from_weight, y0,
     flow_next, p_prev, w0_next, y_prev, w1_next,
@@ -256,8 +256,6 @@
     load_weight.wait()
     from_weight[0] = jnp.zeros_like(from_weight[0])
     put(0, lanes(flow[...] * flow[...]))
-    put(8, lanes(p0[...] * p0[...]))
-    plane[plane_me, pl.ds(11, 5), :] = jnp.zeros((5, 128), F32)
 
     def near_pairs():
         pairs = []
@@ -302,7 +300,13 @@
         )
         for copy, _ in near_copies:
             copy.start()
+
+    def v0_sums():
+        put(1, lanes(grad[...] * flow[...]))
         put(3, lanes(v[...] * v[...]))
+        put(4, lanes(grad[...] * v[...]))
+        put(8, lanes(p0[...] * p0[...]))
+        plane[plane_me, pl.ds(11, 5), :] = jnp.zeros((5, 128), F32)
 
     def own_ratio():
         for _, copy in near_copies[: space_count - 1]:
@@ -331,6 +335,7 @@
             return flux
 
         put(10, lax.fori_loop(0, steps, body, jnp.zeros((1, 128), F32)))
+        v0_sums()
 
     @pl.when(jnp.logical_not(second))
     def _():
@@ -344,13 +349,11 @@
         put(10, lax.fori_loop(0, steps, body, jnp.zeros((1, 128), F32)))
         begin_v0()
         tangent_sweep(from_v, 0, steps)
+        v0_sums()
         c0 = own_ratio()
         for part, copy in zip(parts, send_y0):
             y0[part, :] = from_v[steps, part, :] - c0 * from_flow[steps, part, :]
             copy.start()
-
-    put(1, lanes(grad[...] * flow[...]))
-    put(4, lanes(grad[...] * v[...]))
 
     for _, copy in near_copies[space_count - 1 :]:
         copy.wait_recv()
@@ -368,6 +371,8 @@
     put(9, row)
     adjoint_sweep(from_s1)
     start(send_w1)
+    p0_out[...] = p0[...]
+    s1_out[...] = s1[...]
 
     v1_rows = [jnp.zeros((1, 128), F32)] * 3
     for part, copy in zip(parts, send_y0):
@@ -438,6 +443,11 @@
     from_v[steps] = tangent(steps - 1, from_v[steps - 1] - c1 * from_flow[steps - 1])
     to_before.wait_recv()
     c1_next = total(line_next[7:8])
+    for part, copy in zip(parts, send_w1):
+        copy.wait_recv()
+        s2_out[part, :] = active * (
+            2.0 * s1[part, :] + from_v[steps, part, :] - w1_next[part, :] + c1_next * flow_next[part, :]
+        )
     for _, copy in line_copies:
         copy.wait_recv()
 
@@ -454,14 +464,8 @@
     more = 1.0 + beta
     alpha1 = fresh / (more * more * k0 - 2.0 * alpha0 * more * m11 + alpha0 * alpha0 * k11)
     sens = flux + alpha0 * g0 + alpha1 * (more * g0 - alpha0 * g1)
-    sens_out[...] = jnp.broadcast_to(sens, sens_out.shape)
-
-    along, across = alpha0 + alpha1 * more, alpha1 * alpha0
-    mult_out[...] = along * p0[...] - across * s1[...]
-    for part, copy in zip(parts, send_w1):
-        copy.wait_recv()
-        s2 = 2.0 * s1[part, :] + from_v[steps, part, :] - w1_next[part, :] + c1_next * flow_next[part, :]
-        res_out[part, :] = active * (p0[part, :] - along * s1[part, :] + across * s2)
+    for row, value in enumerate((alpha0 + alpha1 * more, alpha1 * alpha0, sens)):
+        coef_out[pl.ds(row, 1), :] = jnp.broadcast_to(value, (1, 128))
 
     for copies in (send_flow, send_p0, send_w0, send_y0, send_w1):
         for copy in copies:
@@ -471,16 +475,11 @@
     to_before.wait_send()
 
 
-def hand_over(mult_in, res_in, sens_in, mult_out, res_out, sens_out, sems):
-    copies = [
-        pltpu.make_async_copy(mult_in, mult_out, sems.at[0]),
-        pltpu.make_async_copy(res_in, res_out, sems.at[1]),
-    ]
-    for copy in copies:
-        copy.start()
-    sens_out[...] = sens_in[0:1, 0:1]
-    for copy in copies:
-        copy.wait()
+def combine(p0, s1, s2, coef, mult_out, res_out, sens_out):
+    along, across = coef[0:1, 0:1], coef[1:2, 0:1]
+    sens_out[...] = coef[2:3, 0:1]
+    mult_out[...] = along * p0[...] - across * s1[...]
+    res_out[...] = p0[...] - along * s1[...] + across * s2[...]
 
 
 def on_device(rows, axes, advect, growth, forcing, flux_weight, flow_dir, helmholtz):
@@ -498,10 +497,11 @@
         out_shape=(
             pltpu.VMEM((height, width), F32),
             pltpu.VMEM((height, width), F32),
+            pltpu.VMEM((height, width), F32),
             pltpu.VMEM((8, 128), F32),
         ),
         in_specs=[pl.BlockSpec(memory_space=pl.ANY)] * 6,
-        out_specs=tuple([pl.BlockSpec(memory_space=pltpu.VMEM)] * 3),
+        out_specs=tuple([pl.BlockSpec(memory_space=pltpu.VMEM)] * 4),
         scratch_shapes=[
             steps_bf16, steps_bf16, steps_bf16, steps_bf16,
             pltpu.VMEM((height, height), F32), pltpu.VMEM((4, half, half), BF16),
@@ -523,16 +523,15 @@
         flow_dir.reshape(height, width), helmholtz.reshape(height, height),
     )
     mult, res, sens = pl.pallas_call(
-        hand_over,
+        combine,
         out_shape=(
             jax.ShapeDtypeStruct((height, width), F32),
             jax.ShapeDtypeStruct((height, width), F32),
             jax.ShapeDtypeStruct((1, 1), F32),
         ),
-        in_specs=[pl.BlockSpec(memory_space=pl.ANY)] * 2 + [pl.BlockSpec(memory_space=pltpu.VMEM)],
-        out_specs=(pl.BlockSpec(memory_space=pl.ANY),) * 2 + (pl.BlockSpec(memory_space=pltpu.VMEM),),
-        scratch_shapes=[dma((2,))],
-        compiler_params=pltpu.CompilerParams(vmem_limit_bytes=1 << 20),
+        in_specs=[pl.BlockSpec(memory_space=pltpu.VMEM)] * 4,
+        out_specs=(pl.BlockSpec(memory_space=pltpu.VMEM),) * 3,
+        compiler_params=pltpu.CompilerParams(vmem_limit_bytes=4 << 20),
     )(*results)
     return mult[None, None], res[None, None], sens.reshape(())
 

time: 43.8 us -> 43.4 us (level)
  Pallas kernels: 43.1 us -> 42.6 us
where the time goes in v5:
time: 43.4 us; the launch traced here: 43.3 us
  Pallas kernels  42.6 us (98%)
  between operations  0.64 us (1%)
    pallas_call x1, Pallas kernels, on_device(): pl.pallas_call(functools.partial(kernel, (seg_count, space_count, rows)),...  41.4 us
    pallas_call x1, Pallas kernels, on_device(): pl.pallas_call(combine, out_shape=(jax.ShapeDtypeStruct((height, width),...  1.19 us

profile of v5, /device:TPU:1, one launch (start us, length us, event | category | flops | bytes accessed | tf_op | source)
XLA Modules:
  0.0 43.3 jit_solution(16371420460213130910)
XLA Ops:
  0.6 41.4 %shard_map.85 = (f32[256,512]{1,0:T(8,128)S(1)}, f32[256,512]{1,0:T(8,128)S(1)}, f32[256,512]{1,0:T(8,128)S(1)}, f32[8,128]{1,0:T(8,128)S(1)}) custom-call(bf16[4,256,512]{2,1,0:T(8,128)(2,1)} %bitcast.9, bf16[4,256,512]{2,1,0:T(8,128)(2,1)} %bitcast.10, bf16[4,256,512]{2,1,0:T(8,128)(2,1)} %bitcast.11, bf16[4,256,512]{2,1,0:T(8,128)(2,1)} %bitcast.12, ...), custom_call_target="tpu_custom_call" | custom-call | flops 8000000000 | bytes 6000000 | tf_op jit(solution)/shard_map/pallas_call | solution.py:495
  42.1 1.2 %shard_map.86 = (f32[256,512]{1,0:T(8,128)}, f32[256,512]{1,0:T(8,128)}, f32[1,1]{1,0:T(1,128)}) custom-call(f32[256,512]{1,0:T(8,128)S(1)} %get-tuple-element.10.p0, f32[256,512]{1,0:T(8,128)S(1)} %get-tuple-element.11.s1, f32[256,512]{1,0:T(8,128)S(1)} %get-tuple-element.12.s2, f32[8,128]{1,0:T(8,128)S(1)} %get-tuple-element.13.coef), custom_call_target="tpu_custom_call" | custom-call | tf_op jit(solution)/shard_map/pallas_call | solution.py:525

commit v6 on v5

--- a/solution.py
+++ b/solution.py
@@ -12,7 +12,7 @@
 F32 = jnp.float32
 BF16 = jnp.bfloat16
 MESH = pl.DeviceIdType.MESH
-CHUNKS = 4
+CHUNKS = 2
 
 
 def cotangent(angle):
@@ -83,9 +83,9 @@
     advect, growth, forcing, weight, helm, tables, matrix,
     from_p0, from_s1, from_flow, from_v, from_weight, y0,
     flow_next, p_prev, w0_next, y_prev, w1_next,
-    near_own, near_next, plane, line, line_next, coef,
+    near_own, near_next, early, cross, plane, line, line_next, coef,
     load_sem, send_sem, recv_sem,
-    near_send, near_recv, next_recv, plane_send, plane_recv, line_send, line_recv, line_next_sem,
+    near_send, near_recv, next_recv, cross_send, cross_recv, plane_send, plane_recv, line_send, line_recv, line_next_sem,
 ):
     seg_count, space_count, rows = groups
     seg, space = lax.axis_index("seg"), lax.axis_index("space")
@@ -202,6 +202,17 @@
             update = update + forcing[n].astype(F32)
         return mix(forward(), update)
 
+    def tangent_pair(n, one, two):
+        rate = growth[n].astype(F32)
+        speed = advect[n].astype(F32)
+        slopes = derive(jnp.concatenate([one, two], axis=0), [tables[k] for k in range(4)])
+        updates = [
+            now + rate * now - speed * slope
+            for now, slope in ((one, slopes[:height]), (two, slopes[height:]))
+        ]
+        ends = mix(forward(), jnp.concatenate(updates, axis=1))
+        return ends[:, :width], ends[:, width:]
+
     def adjoint_rest(n, pulled):
         rate = growth[n].astype(F32)
         speed = advect[n].astype(F32)
@@ -257,35 +268,40 @@
     from_weight[0] = jnp.zeros_like(from_weight[0])
     put(0, lanes(flow[...] * flow[...]))
 
-    def near_pairs():
-        pairs = []
-        for d in range(1, 2 * space_count):
-            own = d < space_count
+    def near_copy(source, kept, slot, send, receive, to):
+        return pltpu.make_async_remote_copy(
+            src_ref=source, dst_ref=kept.at[slot], send_sem=send, recv_sem=receive.at[slot],
+            device_id=to, device_id_type=MESH,
+        )
+
+    def near_group(source, kept, sends, receive, seg_to, first):
+        group = []
+        for d in range(first, space_count):
             j = lax.rem(space + d, space_count)
-            kept, sems = (near_own, near_recv) if own else (near_next, next_recv)
-            to = (seg if own else before, j)
-            pairs.append(
-                (
-                    pltpu.make_async_remote_copy(
-                        src_ref=near_own.at[space], dst_ref=kept.at[space], send_sem=near_send.at[d - 1],
-                        recv_sem=sems.at[space], device_id=to, device_id_type=MESH,
-                    ),
-                    pltpu.make_async_remote_copy(
-                        src_ref=near_own.at[space], dst_ref=kept.at[j], send_sem=near_send.at[d - 1],
-                        recv_sem=sems.at[j], device_id=to, device_id_type=MESH,
-                    ),
-                )
-            )
-        return pairs
-
-    near_copies = near_pairs()
-
-    def near_ratio(row, kept):
+            group.append([near_copy(source, kept, s, sends.at[d], receive, (seg_to, j)) for s in (space, j)])
+        return group
+
+    own_tile = near_own.at[space]
+    own_copies = near_group(own_tile, near_own, near_send.at[0], near_recv, seg, 1)
+    v0_copies = near_group(own_tile, near_next, near_send.at[1], next_recv, before, 0)
+    w0_copies = near_group(early, near_next, near_send.at[1], next_recv, before, 0)
+    cross_copies = near_group(cross.at[space], cross, cross_send, cross_recv, seg, 1)
+
+    def near_ratio(row, kept, less=None):
         sums = kept[0]
         for x in range(1, space_count):
             sums = sums + kept[x]
-        c = total(sums[1:2]) / (total(sums[0:1]) + EPS)
+        top = total(sums[1:2])
+        if less is not None:
+            rows_less = less[0]
+            for x in range(1, space_count):
+                rows_less = rows_less + less[x]
+            top = top - total(rows_less[1:2])
+        c = top / (total(sums[0:1]) + EPS)
         coef[pl.ds(row, 1), :] = jnp.broadcast_to(c, (1, 128))
+
+    def flow_tile(row):
+        return jnp.concatenate([plane[plane_me, pl.ds(0, 1), :], row, jnp.zeros((6, 128), F32)], axis=0)
 
     def begin_v0():
         row = jnp.zeros((1, 128), F32)
@@ -295,10 +311,8 @@
             v[part, :] = piece_of
             row = row + lanes(flow[part, :] * piece_of)
         put(2, row)
-        near_own[space] = jnp.concatenate(
-            [plane[plane_me, pl.ds(0, 1), :], row, jnp.zeros((6, 128), F32)], axis=0
-        )
-        for copy, _ in near_copies:
+        near_own[space] = flow_tile(row)
+        for copy, _ in own_copies:
             copy.start()
 
     def v0_sums():
@@ -309,7 +323,7 @@
         plane[plane_me, pl.ds(11, 5), :] = jnp.zeros((5, 128), F32)
 
     def own_ratio():
-        for _, copy in near_copies[: space_count - 1]:
+        for _, copy in own_copies:
             copy.wait_recv()
         near_ratio(0, near_own)
         return coef[0:1, 0:1]
@@ -319,15 +333,21 @@
     @pl.when(second)
     def _():
         begin_v0()
+        for copy, _ in v0_copies:
+            copy.start()
 
         @pl.loop(0, steps - 1)
         def _(n):
-            one, two = tangent(n, from_v[n]), tangent(n, from_flow[n])
+            one, two = tangent_pair(n, from_v[n], from_flow[n])
             from_v[n + 1] = one
             from_flow[n + 1] = two
 
         y0[...] = tangent(steps - 1, from_v[steps - 1] - own_ratio() * from_flow[steps - 1])
         start(send_y0)
+        arrived(send_flow)
+        cross[space] = flow_tile(lanes(flow_next[...] * p0[...]))
+        for copy, _ in cross_copies:
+            copy.start()
 
         def body(k, flux):
             now, flux = gradient_step(k, flux)
@@ -336,9 +356,16 @@
 
         put(10, lax.fori_loop(0, steps, body, jnp.zeros((1, 128), F32)))
         v0_sums()
+        for _, copy in v0_copies + cross_copies:
+            copy.wait_recv()
+        near_ratio(1, near_next, less=cross)
 
     @pl.when(jnp.logical_not(second))
     def _():
+        early[...] = flow_tile(lanes(flow[...] * w0[...]))
+        for copy, _ in w0_copies:
+            copy.start()
+
         def body(k, flux):
             one = tangent(k, from_flow[k])
             now, flux = gradient_step(k, flux)
@@ -354,12 +381,12 @@
         for part, copy in zip(parts, send_y0):
             y0[part, :] = from_v[steps, part, :] - c0 * from_flow[steps, part, :]
             copy.start()
-
-    for _, copy in near_copies[space_count - 1 :]:
-        copy.wait_recv()
-    near_ratio(1, near_next)
+        for _, copy in v0_copies:
+            copy.wait_recv()
+        near_ratio(1, near_next)
+        arrived(send_flow)
+
     c0, c0_next = coef[0:1, 0:1], coef[1:2, 0:1]
-    arrived(send_flow)
     row = jnp.zeros((1, 128), F32)
     for part, copy in zip(parts, send_w0):
         copy.wait_recv()
@@ -470,8 +497,14 @@
     for copies in (send_flow, send_p0, send_w0, send_y0, send_w1):
         for copy in copies:
             copy.wait_send()
-    for copy, _ in near_copies + plane_copies + line_copies:
+    for copy, _ in own_copies + v0_copies + plane_copies + line_copies:
         copy.wait_send()
+
+    @pl.when(second)
+    def _():
+        for copy, _ in cross_copies:
+            copy.wait_send()
+
     to_before.wait_send()
 
 
@@ -509,9 +542,10 @@
             *[pltpu.VMEM((steps + 1, height, width), F32)] * 5, field,
             *[field] * 5,
             pltpu.VMEM((space_count, 8, 128), F32), pltpu.VMEM((space_count, 8, 128), F32),
+            pltpu.VMEM((8, 128), F32), pltpu.VMEM((space_count, 8, 128), F32),
             pltpu.VMEM((plane_size, 16, 128), F32), pltpu.VMEM((rows, 8, 128), F32), pltpu.VMEM((8, 128), F32), pltpu.VMEM((8, 128), F32),
             dma((3 * steps + 3,)), dma((5, CHUNKS)), dma((5, CHUNKS)),
-            dma((2 * space_count - 1,)), dma((space_count,)), dma((space_count,)),
+            dma((2, space_count)), dma((space_count,)), dma((space_count,)), dma((space_count,)), dma((space_count,)),
             dma((plane_size,)), dma((plane_size,)), dma((rows,)), dma((rows,)), dma,
         ],
         compiler_params=pltpu.CompilerParams(

time: 43.4 us -> 43.2 us (level)
  no operation moved by 1% of the time
where the time goes in v6:
time: 43.2 us
  Pallas kernels  42.5 us (98%)
  between operations  0.64 us (1%)
    pallas_call x1, Pallas kernels, on_device(): pl.pallas_call(functools.partial(kernel, (seg_count, space_count, rows)),...  41.3 us
    pallas_call x1, Pallas kernels, on_device(): pl.pallas_call(combine, out_shape=(jax.ShapeDtypeStruct((height, width),...  1.19 us

profile of v6, /device:TPU:1, one launch (start us, length us, event | category | flops | bytes accessed | tf_op | source)
XLA Modules:
  0.0 43.2 jit_solution(10472271612366663376)
XLA Ops:
  0.6 41.3 %shard_map.85 = (f32[256,512]{1,0:T(8,128)S(1)}, f32[256,512]{1,0:T(8,128)S(1)}, f32[256,512]{1,0:T(8,128)S(1)}, f32[8,128]{1,0:T(8,128)S(1)}) custom-call(bf16[4,256,512]{2,1,0:T(8,128)(2,1)} %bitcast.9, bf16[4,256,512]{2,1,0:T(8,128)(2,1)} %bitcast.10, bf16[4,256,512]{2,1,0:T(8,128)(2,1)} %bitcast.11, bf16[4,256,512]{2,1,0:T(8,128)(2,1)} %bitcast.12, ...), custom_call_target="tpu_custom_call" | custom-call | flops 8000000000 | bytes 6000000 | tf_op jit(solution)/shard_map/pallas_call | solution.py:528
  42.0 1.2 %shard_map.86 = (f32[256,512]{1,0:T(8,128)}, f32[256,512]{1,0:T(8,128)}, f32[1,1]{1,0:T(1,128)}) custom-call(f32[256,512]{1,0:T(8,128)S(1)} %get-tuple-element.10.p0, f32[256,512]{1,0:T(8,128)S(1)} %get-tuple-element.11.s1, f32[256,512]{1,0:T(8,128)S(1)} %get-tuple-element.12.s2, f32[8,128]{1,0:T(8,128)S(1)} %get-tuple-element.13.coef), custom_call_target="tpu_custom_call" | custom-call | tf_op jit(solution)/shard_map/pallas_call | solution.py:559
